TPU v7x, 256 devices: a whole 4x4x8 slice. The times are simulated.
256 devices in a mesh: shard: 128 (over y, x, z), rep: 2 (over core).
Axes of the slice: x: 4, y: 4, z: 8, core: 2. Of those that a mesh axis runs over, the one named last changes fastest.
Arguments:
- embeddings: bfloat16 [131072, 1024], P('shard')
- labels: int32 [131072], P('shard'), may hold values from 0 to 2047, as said below
Outputs:
- density: float32 [131072], P('shard')
Inputs may be any that keep to these rules, and one draw needn't show every extreme that they name: `labels`: in each aligned block of 1024 documents (those of one index of shard) at most 1 name any one cluster, and in every block some cluster is named by exactly 1; so a cluster holds at most 128 documents, and some cluster holds exactly 128.
All inputs are finite; a program needn't handle non-finite values.
Results may differ from a plain program's by a relative error of at most 0.00038.
Values may be sent and summed in bfloat16 or wider, within the bound.
A program may use at most 64 MiB of HBM per device.

v0:
```python
import jax
import jax.numpy as jnp
from jax import lax
from jax.sharding import PartitionSpec as P

CL_DEV = 16
CAP = 128


sharpness = 4.0
epsilon = 1e-06


def unit_rows(embeddings):
    values = embeddings.astype(jnp.float32)
    scale = lax.rsqrt(jnp.sum(values * values, axis=-1, keepdims=True) + epsilon)
    return (values * scale).astype(jnp.bfloat16)


def slot_ranks(labels):
    doc_order = jnp.argsort(labels, stable=True)
    sorted_labels = labels[doc_order]
    first_seen = jnp.searchsorted(sorted_labels, sorted_labels, side="left")
    sorted_rank = jnp.arange(labels.shape[0], dtype=jnp.int32) - first_seen
    return jnp.zeros_like(labels).at[doc_order].set(sorted_rank)


def cluster_sums(cluster_rows, cluster_marks):
    gram = jnp.einsum("rd,cd->rc", cluster_rows, cluster_rows, preferred_element_type=jnp.float32)
    weights = jnp.exp(sharpness * (gram - 1.0)) * cluster_marks.astype(jnp.float32)[None, :]
    row_ids = lax.broadcasted_iota(jnp.int32, gram.shape, 0)
    col_ids = lax.broadcasted_iota(jnp.int32, gram.shape, 1)
    weights = jnp.where(row_ids == col_ids, 0.0, weights)
    return jnp.sum(weights, axis=1)


def local(embeddings, labels):
    shard_count = lax.axis_size("shard")
    rep_count = lax.axis_size("rep")
    rep_index = lax.axis_index("rep")
    slot_count = CAP // shard_count
    width = embeddings.shape[1]
    half_count = CL_DEV // rep_count
    unit = unit_rows(embeddings)
    ranks = slot_ranks(labels)
    owner_id = labels // CL_DEV
    local_id = labels % CL_DEV
    column = owner_id * slot_count + ranks
    outgoing = (
        jnp.zeros((CL_DEV, shard_count * slot_count, width), jnp.bfloat16)
        .at[local_id, column]
        .set(unit)
    )
    presence = (
        jnp.zeros((CL_DEV, shard_count * slot_count), jnp.bfloat16).at[local_id, column].set(1.0)
    )
    got_rows, got_marks = (
        lax.all_to_all(outgoing, "shard", split_axis=1, concat_axis=1, tiled=True),
        lax.all_to_all(presence, "shard", split_axis=1, concat_axis=1, tiled=True),
    )
    tile_rows = lax.dynamic_slice_in_dim(got_rows, rep_index * half_count, half_count, 0)
    tile_marks = lax.dynamic_slice_in_dim(got_marks, rep_index * half_count, half_count, 0)
    partial_sums = lax.map(
        lambda item_pair: cluster_sums(item_pair[0], item_pair[1]), (tile_rows, tile_marks)
    )
    densities = lax.all_gather(partial_sums, "rep", axis=0, tiled=True)
    returned = lax.all_to_all(densities, "shard", split_axis=1, concat_axis=1, tiled=True)
    own_totals = returned[local_id, column]
    return jnp.log1p(own_totals)


def solution(mesh):
    return jax.shard_map(
        local,
        mesh=mesh,
        in_specs=(P("shard", None), P("shard")),
        out_specs=P("shard"),
        check_vma=False,
    )
```

profile of v0, /device:TPU:1, one launch (start us, length us, event | category | flops | bytes accessed | tf_op | source)
XLA Modules:
  0.0 251.7 jit_solution(14771647097224989652)
XLA Ops:
  0.0 5.1 %sort.17 = (s32[1024]{0:T(1024)}, s32[1024]{0:T(1024)S(1)}) sort(s32[1024]{0:T(1024)} %param.7, s32[1024]{0:T(1024)S(1)} %iota.23), dimensions={0}, to_apply=%region_0.0 | sort | flops 10240 | bytes 16384 | tf_op jit(solution)/shard_map/jit(argsort)/sort | solution.py:21
  5.1 5.7 %gather_fusion.1 = s32[1024]{0:T(1024)S(1)} fusion(s32[1024]{0:T(1024)} %param.7, s32[1024]{0:T(1024)S(1)} %get-tuple-element.176), kind=kCustom, calls=%fused_computation.1 | custom fusion | bytes 12288 | tf_op jit(solution)/shard_map/gather | solution.py:22
  10.8 50.7 %while.38 = (s32[]{:T(128)}, u32[1024]{0:T(1024)S(1)}, u32[1024]{0:T(1024)S(1)}, s32[1024]{0:T(1024)S(1)}, s32[]{:T(128)}, /*index=5*/s32[]{:T(128)}, s32[]{}) while((s32[]{:T(128)}, u32[1024]{0:T(1024)S(1)}, u32[1024]{0:T(1024)S(1)}, s32[1024]{0:T(1024)S(1)}, s32[]{:T(128)}, /*index=5*/s32[]{:T(128)}, s32[]{}) %tuple.62), condition=%wide.region_2.3_spmd.clone, body=%wide.region_1.0_spmd.clone.sunk | while | flops 19460 | bytes 67685 | solution.py:23
  10.9 4.5 %gather_fusion = s32[1024]{0:T(1024)S(1)} fusion(s32[1024]{0:T(1024)S(1)} %get-tuple-element.249, u32[1024]{0:T(1024)S(1)} %broadcast_clamp_fusion.3), kind=kCustom, calls=%fused_computation.clone.clone.1 | custom fusion | bytes 12288 | tf_op jit(solution)/shard_map/jit(searchsorted)/jit(_searchsorted_scan_impl)/vmap(jit(_searchsorted_scan_impl))/while/body/eval_jaxpr/gather | solution.py:23
  15.5 4.5 %gather_fusion = s32[1024]{0:T(1024)S(1)} fusion(s32[1024]{0:T(1024)S(1)} %get-tuple-element.249, u32[1024]{0:T(1024)S(1)} %broadcast_clamp_fusion.3), kind=kCustom, calls=%fused_computation.clone.clone.1 | custom fusion | bytes 12288 | tf_op jit(solution)/shard_map/jit(searchsorted)/jit(_searchsorted_scan_impl)/vmap(jit(_searchsorted_scan_impl))/while/body/eval_jaxpr/gather | solution.py:23
  20.1 4.5 %gather_fusion = s32[1024]{0:T(1024)S(1)} fusion(s32[1024]{0:T(1024)S(1)} %get-tuple-element.249, u32[1024]{0:T(1024)S(1)} %broadcast_clamp_fusion.3), kind=kCustom, calls=%fused_computation.clone.clone.1 | custom fusion | bytes 12288 | tf_op jit(solution)/shard_map/jit(searchsorted)/jit(_searchsorted_scan_impl)/vmap(jit(_searchsorted_scan_impl))/while/body/eval_jaxpr/gather | solution.py:23
  24.7 4.5 %gather_fusion = s32[1024]{0:T(1024)S(1)} fusion(s32[1024]{0:T(1024)S(1)} %get-tuple-element.249, u32[1024]{0:T(1024)S(1)} %broadcast_clamp_fusion.3), kind=kCustom, calls=%fused_computation.clone.clone.1 | custom fusion | bytes 12288 | tf_op jit(solution)/shard_map/jit(searchsorted)/jit(_searchsorted_scan_impl)/vmap(jit(_searchsorted_scan_impl))/while/body/eval_jaxpr/gather | solution.py:23
  29.3 4.5 %gather_fusion = s32[1024]{0:T(1024)S(1)} fusion(s32[1024]{0:T(1024)S(1)} %get-tuple-element.249, u32[1024]{0:T(1024)S(1)} %broadcast_clamp_fusion.3), kind=kCustom, calls=%fused_computation.clone.clone.1 | custom fusion | bytes 12288 | tf_op jit(solution)/shard_map/jit(searchsorted)/jit(_searchsorted_scan_impl)/vmap(jit(_searchsorted_scan_impl))/while/body/eval_jaxpr/gather | solution.py:23
  33.9 4.5 %gather_fusion = s32[1024]{0:T(1024)S(1)} fusion(s32[1024]{0:T(1024)S(1)} %get-tuple-element.249, u32[1024]{0:T(1024)S(1)} %broadcast_clamp_fusion.3), kind=kCustom, calls=%fused_computation.clone.clone.1 | custom fusion | bytes 12288 | tf_op jit(solution)/shard_map/jit(searchsorted)/jit(_searchsorted_scan_impl)/vmap(jit(_searchsorted_scan_impl))/while/body/eval_jaxpr/gather | solution.py:23
  38.5 4.5 %gather_fusion = s32[1024]{0:T(1024)S(1)} fusion(s32[1024]{0:T(1024)S(1)} %get-tuple-element.249, u32[1024]{0:T(1024)S(1)} %broadcast_clamp_fusion.3), kind=kCustom, calls=%fused_computation.clone.clone.1 | custom fusion | bytes 12288 | tf_op jit(solution)/shard_map/jit(searchsorted)/jit(_searchsorted_scan_impl)/vmap(jit(_searchsorted_scan_impl))/while/body/eval_jaxpr/gather | solution.py:23
  43.2 4.5 %gather_fusion = s32[1024]{0:T(1024)S(1)} fusion(s32[1024]{0:T(1024)S(1)} %get-tuple-element.249, u32[1024]{0:T(1024)S(1)} %broadcast_clamp_fusion.3), kind=kCustom, calls=%fused_computation.clone.clone.1 | custom fusion | bytes 12288 | tf_op jit(solution)/shard_map/jit(searchsorted)/jit(_searchsorted_scan_impl)/vmap(jit(_searchsorted_scan_impl))/while/body/eval_jaxpr/gather | solution.py:23
  47.8 4.5 %gather_fusion = s32[1024]{0:T(1024)S(1)} fusion(s32[1024]{0:T(1024)S(1)} %get-tuple-element.249, u32[1024]{0:T(1024)S(1)} %broadcast_clamp_fusion.3), kind=kCustom, calls=%fused_computation.clone.clone.1 | custom fusion | bytes 12288 | tf_op jit(solution)/shard_map/jit(searchsorted)/jit(_searchsorted_scan_impl)/vmap(jit(_searchsorted_scan_impl))/while/body/eval_jaxpr/gather | solution.py:23
  52.4 4.5 %gather_fusion = s32[1024]{0:T(1024)S(1)} fusion(s32[1024]{0:T(1024)S(1)} %get-tuple-element.249, u32[1024]{0:T(1024)S(1)} %broadcast_clamp_fusion.3), kind=kCustom, calls=%fused_computation.clone.clone.1 | custom fusion | bytes 12288 | tf_op jit(solution)/shard_map/jit(searchsorted)/jit(_searchsorted_scan_impl)/vmap(jit(_searchsorted_scan_impl))/while/body/eval_jaxpr/gather | solution.py:23
  57.0 4.5 %gather_fusion = s32[1024]{0:T(1024)S(1)} fusion(s32[1024]{0:T(1024)S(1)} %get-tuple-element.249, u32[1024]{0:T(1024)S(1)} %broadcast_clamp_fusion.3), kind=kCustom, calls=%fused_computation.clone.clone.1 | custom fusion | bytes 12288 | tf_op jit(solution)/shard_map/jit(searchsorted)/jit(_searchsorted_scan_impl)/vmap(jit(_searchsorted_scan_impl))/while/body/eval_jaxpr/gather | solution.py:23
  66.2 7.6 %scatter_custom_fusion.2 = bf16[2048]{0:T(1024)(128)(2,1)S(1)} fusion(s32[1024]{0:T(1024)S(1)} %broadcast_select_fusion, bf16[1024]{0:T(1024)(128)(2,1)S(1)} %broadcast.71, bf16[]{:T(256)} %constant.106.clone.1), kind=kCustom, calls=%fused_computation.47 | custom fusion | bytes 4098
  74.5 16.5 %all-to-all-start.1 = ((bf16[16,128,1]{0,2,1:T(2,128)(2,1)}), bf16[16,128,1]{0,2,1:T(2,128)(2,1)S(1)}, u32[]{:S(2)}, u32[]{:S(2)}) async-start(bf16[16,128,1]{0,2,1:T(2,128)(2,1)} %copy.14), calls=%async_computation.1 | async-start | bytes 131072 | tf_op jit(solution)/shard_map/all_to_all | solution.py:59
  91.5 8.3 %scatter_custom_fusion.1 = bf16[2048,1024]{1,0:T(8,128)(2,1)} fusion(s32[1024]{0:T(1024)S(1)} %broadcast_select_fusion, bf16[1024,1024]{1,0:T(8,128)(2,1)S(1)} %copy-done.1, bf16[]{:T(256)} %constant.106.clone.1, f32[1024]{0:T(1024)S(1)} %add_rsqrt_fusion), kind=kCustom, calls=%fused_computation.25 | custom fusion | flops 3145728 | bytes 6295554
  99.9 6.4 %copy.13 = bf16[16,128,1024]{2,0,1:T(8,128)(2,1)} copy(bf16[16,128,1024]{2,1,0:T(8,128)(2,1)} %bitcast.26) | data formatting | bytes 8388608 | tf_op jit(solution)/shard_map/scatter | solution.py:52
  106.3 13.6 %all-to-all-start = ((bf16[16,128,1024]{2,0,1:T(8,128)(2,1)}), bf16[16,128,1024]{2,0,1:T(8,128)(2,1)}, u32[]{:S(2)}, u32[]{:S(2)}) async-start(bf16[16,128,1024]{2,0,1:T(8,128)(2,1)} %copy.13), calls=%async_computation | async-start | bytes 8388608 | tf_op jit(solution)/shard_map/all_to_all | solution.py:58
  120.2 95.6 %all-to-all-done = bf16[16,128,1024]{2,0,1:T(8,128)(2,1)} async-done(((bf16[16,128,1024]{2,0,1:T(8,128)(2,1)}), bf16[16,128,1024]{2,0,1:T(8,128)(2,1)}, u32[]{:S(2)}, u32[]{:S(2)}) %all-to-all-start) | async-done | bytes 4194336 | tf_op jit(solution)/shard_map/all_to_all | solution.py:58
  221.2 5.5 %all_gather.3 = f32[16,128]{1,0:T(8,128)S(1)} all-gather(f32[8,128]{1,0:T(8,128)S(1)} %get-tuple-element.128), channel_id=1, replica_groups=mesh['shard'=128,'rep'=2] {'rep'}, dimensions={0}, use_global_device_ids=true | all-gather | bytes 12288 | tf_op jit(solution)/shard_map/all_gather | solution.py:66
  227.5 6.2 %all-to-all-start.2 = ((f32[16,128,1]{0,2,1:T(1,128)}), f32[16,128,1]{0,2,1:T(1,128)S(1)}, u32[]{:S(2)}, u32[]{:S(2)}) async-start(f32[16,128,1]{0,2,1:T(1,128)} %copy.17), calls=%async_computation.2 | async-start | bytes 131072 | tf_op jit(solution)/shard_map/all_to_all | solution.py:67
  233.7 10.5 %all-to-all-done.2 = f32[16,128,1]{0,2,1:T(1,128)S(1)} async-done(((f32[16,128,1]{0,2,1:T(1,128)}), f32[16,128,1]{0,2,1:T(1,128)S(1)}, u32[]{:S(2)}, u32[]{:S(2)}) %all-to-all-start.2) | async-done | bytes 8224 | tf_op jit(solution)/shard_map/all_to_all | solution.py:67
  244.3 6.8 %gather_fusion.2 = f32[1024]{0:T(1024)S(1)} fusion(f32[16,128]{1,0:T(8,128)S(1)} %bitcast.24, s32[1024]{0:T(1024)S(1)} %bitcast.25), kind=kCustom, calls=%fused_computation.2 | custom fusion | bytes 16384 | tf_op jit(solution)/shard_map/gather | solution.py:68
  (101 shorter events, 15.7 us)
Async XLA Ops:
  10.8 55.1 %copy-start = (s32[1024]{0:T(1024)S(1)}, s32[1024]{0:T(1024)}, u32[]{:S(2)}) copy-start(s32[1024]{0:T(1024)} %param.7) | copy-start | bytes 12292
  10.8 55.1 %copy-start.3 = (s32[2]{0:T(128)S(1)}, s32[2]{0:T(128)}, u32[]{:S(2)}) copy-start(s32[2]{0:T(128)} %constant.123) | copy-start | bytes 28
  10.8 55.2 %copy-start.2 = (s32[2]{0:T(128)S(1)}, s32[2]{0:T(128)}, u32[]{:S(2)}) copy-start(s32[2]{0:T(128)} %constant.120) | copy-start | bytes 28
  10.8 80.2 %copy-start.1 = (bf16[1024,1024]{1,0:T(8,128)(2,1)S(1)}, bf16[1024,1024]{1,0:T(8,128)(2,1)}, u32[]{:S(2)}) copy-start(bf16[1024,1024]{1,0:T(8,128)(2,1)} %param.6) | copy-start | bytes 6291460
  74.5 31.8 %all-to-all-start.1 = ((bf16[16,128,1]{0,2,1:T(2,128)(2,1)}), bf16[16,128,1]{0,2,1:T(2,128)(2,1)S(1)}, u32[]{:S(2)}, u32[]{:S(2)}) async-start(bf16[16,128,1]{0,2,1:T(2,128)(2,1)} %copy.14), calls=%async_computation.1 | async-start | bytes 131072 | tf_op jit(solution)/shard_map/all_to_all | solution.py:59
  106.3 109.4 %all-to-all-start = ((bf16[16,128,1024]{2,0,1:T(8,128)(2,1)}), bf16[16,128,1024]{2,0,1:T(8,128)(2,1)}, u32[]{:S(2)}, u32[]{:S(2)}) async-start(bf16[16,128,1024]{2,0,1:T(8,128)(2,1)} %copy.13), calls=%async_computation | async-start | bytes 8388608 | tf_op jit(solution)/shard_map/all_to_all | solution.py:58
  227.5 16.7 %all-to-all-start.2 = ((f32[16,128,1]{0,2,1:T(1,128)}), f32[16,128,1]{0,2,1:T(1,128)S(1)}, u32[]{:S(2)}, u32[]{:S(2)}) async-start(f32[16,128,1]{0,2,1:T(1,128)} %copy.17), calls=%async_computation.2 | async-start | bytes 131072 | tf_op jit(solution)/shard_map/all_to_all | solution.py:67
where the time goes:
time: 252 us
  waiting for transfers between devices  106 us (42%)
  local copies, waits for them, and re-layouts  86.3 us (34%)
  starting transfers between devices  36.3 us (14%)
  other arithmetic  14.5 us (6%)
  blocking collectives  5.53 us (2%)
    all_to_all x1, waiting for transfers between devices, local(): lax.all_to_all(outgoing, 'shard', split_axis=1, concat_axis=1, tiled=True)  95.6 us
    gather x11, local copies, waits for them, and re-layouts, slot_ranks(): first_seen = jnp.searchsorted(sorted_labels, sorted_labels, side='left')  49.8 us
    all_to_all x1, starting transfers between devices, local(): lax.all_to_all(presence, 'shard', split_axis=1, concat_axis=1, tiled=True)  16.5 us
    all_to_all x1, starting transfers between devices, local(): lax.all_to_all(outgoing, 'shard', split_axis=1, concat_axis=1, tiled=True)  13.6 us
    all_to_all x1, waiting for transfers between devices, local(): lax.all_to_all(densities, 'shard', split_axis=1, concat_axis=1, tiled=True)  10.5 us
    unnamed x6, other arithmetic  8.51 us
    unnamed x11, local copies, waits for them, and re-layouts  7.69 us
    gather x1, local copies, waits for them, and re-layouts, local(): own_totals = returned[local_id, column]  6.81 us
  transfers between devices with their start and end apart: 3, of which 2 were waited for; matrix products, arithmetic and copies ran while one was open for 6% of the time, Pallas kernels for 0%

commit v1 on v0

v1 whole, which is shorter than its diff:
```python
import functools
import jax
import jax.numpy as jnp
from jax import lax
from jax.experimental import pallas as pl
from jax.experimental.pallas import tpu as pltpu
from jax.sharding import PartitionSpec as P

SHARDS = 128
DOCS_DEV = 1024
D = 1024
CL = 8
GROUPS = 4
GROUP_Q = SHARDS // GROUPS
ROWS = GROUP_Q * CL

sharpness = 4.0
epsilon = 1e-06


def offset_of(q):
    k = q % 8
    dz = jnp.where(k % 2 == 1, (k + 1) // 2, (8 - k // 2) % 8)
    return (q // 32) % 4, (q // 8) % 4, dz


def q_of(dy, dx, dz):
    k = jnp.where(dz == 0, 0, jnp.where(dz <= 4, 2 * dz - 1, 2 * (8 - dz)))
    return dy * 32 + dx * 8 + k


def shift(s, q, sign):
    dy, dx, dz = offset_of(q)
    y = (s // 32 + 4 + sign * dy) % 4
    x = (s // 8 % 4 + 4 + sign * dx) % 4
    z = (s % 8 + 8 + sign * dz) % 8
    return y * 32 + x * 8 + z


def kernel(e_hbm, labels_ref, out_ref, e_ref, send, recv, unit, tot, ret, halves,
           load_sem, send_sem, recv_sem, back_send, back_recv, half_sem):
    me = lax.axis_index("shard")
    rep = lax.axis_index("rep")
    load = pltpu.make_async_copy(e_hbm, e_ref, load_sem)
    load.start()

    barrier = pltpu.get_barrier_semaphore()

    def greet(q, _):
        pl.semaphore_signal(barrier, inc=1, device_id={"shard": shift(me, q, -1)})
        return 0

    lax.fori_loop(1, SHARDS, greet, 0)
    pl.semaphore_signal(barrier, inc=1, device_id={"rep": 1 - rep})
    load.wait()

    labels = labels_ref[...]
    owner = labels // 16
    dy = (owner // 32 - me // 32 + 4) % 4
    dx = (owner // 8 % 4 - me // 8 % 4 + 4) % 4
    dz = (owner % 8 - me % 8 + 8) % 8
    doc_q = q_of(dy, dx, dz)
    doc_slot = jnp.where(labels % 16 // 8 == rep, doc_q * 8 + labels % 8, -1)

    def row_copy(q):
        return pltpu.make_async_remote_copy(
            src_ref=send.at[q], dst_ref=recv.at[q], send_sem=send_sem,
            recv_sem=recv_sem.at[q // GROUP_Q],
            device_id={"shard": shift(me, q, 1)})

    def back_copy(q):
        return pltpu.make_async_remote_copy(
            src_ref=tot.at[q // 16], dst_ref=ret.at[q], send_sem=back_send,
            recv_sem=back_recv, device_id={"shard": shift(me, q, -1)})

    def fill(g):
        ids = lax.broadcasted_iota(jnp.int32, (ROWS, 128), 0) + g * ROWS
        hits = [ids == doc_slot[j:j + 1, :] for j in range(8)]
        onehot = jnp.concatenate(
            [jnp.where(h, 1.0, 0.0).astype(jnp.bfloat16) for h in hits], axis=1)
        any_hit = functools.reduce(
            jnp.add, [jnp.where(h, 1.0, 0.0) for h in hits])
        present = jnp.sum(any_hit, axis=1, keepdims=True) > 0.0
        rows = jnp.dot(onehot, e_ref[...], preferred_element_type=jnp.float32)
        rows = jnp.where(present, rows, jnp.nan)
        rows = rows.reshape(GROUP_Q, CL, D).astype(jnp.bfloat16)
        send[g * GROUP_Q:(g + 1) * GROUP_Q] = rows
        if g == 0:
            recv[0] = rows[0]

    for g in range(GROUPS):
        fill(g)
        if g == 0:
            pl.semaphore_wait(barrier, SHARDS)

        def push(q, _):
            row_copy(q).start()
            return 0

        lax.fori_loop(1 if g == 0 else g * GROUP_Q, (g + 1) * GROUP_Q, push, 0)

    row_id = lax.broadcasted_iota(jnp.int32, (ROWS, ROWS), 0)
    col_id = lax.broadcasted_iota(jnp.int32, (ROWS, ROWS), 1)
    same = row_id % CL == col_id % CL
    same_off = same & (row_id != col_id)

    def weights(a, b, mask):
        gram = lax.dot_general(a, b, (((1,), (1,)), ((), ())),
                               preferred_element_type=jnp.float32)
        ok = mask & (gram == gram)
        w = jnp.where(ok, jnp.exp(sharpness * (gram - 1.0)), 0.0)
        return jnp.sum(w, axis=0, keepdims=True)

    totals = [jnp.zeros((1, ROWS), jnp.float32) for _ in range(GROUPS)]
    for g in range(GROUPS):
        lo = 1 if g == 0 else g * GROUP_Q
        block = pl.ds(lo, (g + 1) * GROUP_Q - lo)
        pltpu.make_async_copy(recv.at[block], recv.at[block], recv_sem.at[g]).wait()
        values = recv[g * GROUP_Q:(g + 1) * GROUP_Q].astype(jnp.float32).reshape(ROWS, D)
        scale = lax.rsqrt(jnp.sum(values * values, axis=1, keepdims=True) + epsilon)
        mine = (values * scale).astype(jnp.bfloat16)
        unit[g * ROWS:(g + 1) * ROWS] = mine
        totals[g] += weights(mine, mine, same_off)
        for h in range(g):
            other = unit[h * ROWS:(h + 1) * ROWS]
            totals[g] += weights(other, mine, same)
            totals[h] += weights(mine, other, same)

    for j in range(8):
        g, part = j // 2, j % 2
        tot[j] = totals[g][:, part * 128:(part + 1) * 128]
    ret[0] = tot[0]

    def push_back(q, _):
        back_copy(q).start()
        return 0

    lax.fori_loop(1, SHARDS, push_back, 0)
    everything = pl.ds(1, SHARDS - 1)
    pltpu.make_async_copy(ret.at[everything], ret.at[everything], back_recv).wait()

    got = ret[...].reshape(SHARDS, 128)
    q_id = lax.broadcasted_iota(jnp.int32, (SHARDS, 128), 0)
    lane = lax.broadcasted_iota(jnp.int32, (SHARDS, 128), 1)
    got = jnp.where(lane // CL == q_id % 16, got, 0.0).T
    halves[rep] = jnp.sum(got.reshape(16, CL, 128), axis=0)
    swap = pltpu.make_async_remote_copy(
        src_ref=halves.at[rep], dst_ref=halves.at[rep], send_sem=half_sem.at[0],
        recv_sem=half_sem.at[1], device_id={"rep": 1 - rep})
    swap.start()
    swap.wait()

    value = jnp.zeros((8, 128), jnp.float32)
    cluster = labels % 16
    for c in range(16):
        line = jnp.broadcast_to(halves[c // 8, c % 8:c % 8 + 1, :], (8, 128))
        value = jnp.where(cluster == c, jnp.take_along_axis(line, doc_q, axis=1), value)
    out_ref[...] = value

    pltpu.make_async_copy(send.at[everything], send.at[everything], send_sem).wait()
    pltpu.make_async_copy(ret.at[everything], ret.at[everything], back_send).wait()


def local(embeddings, labels):
    totals = pl.pallas_call(
        kernel,
        out_shape=jax.ShapeDtypeStruct((8, 128), jnp.float32),
        in_specs=[pl.BlockSpec(memory_space=pl.ANY), pl.BlockSpec(memory_space=pltpu.VMEM)],
        out_specs=pl.BlockSpec(memory_space=pltpu.VMEM),
        scratch_shapes=[
            pltpu.VMEM((DOCS_DEV, D), jnp.bfloat16),
            pltpu.VMEM((SHARDS, CL, D), jnp.bfloat16),
            pltpu.VMEM((SHARDS, CL, D), jnp.bfloat16),
            pltpu.VMEM((SHARDS * CL, D), jnp.bfloat16),
            pltpu.VMEM((8, 1, 128), jnp.float32),
            pltpu.VMEM((SHARDS, 1, 128), jnp.float32),
            pltpu.VMEM((2, 8, 128), jnp.float32),
            pltpu.SemaphoreType.DMA,
            pltpu.SemaphoreType.DMA,
            pltpu.SemaphoreType.DMA((GROUPS,)),
            pltpu.SemaphoreType.DMA,
            pltpu.SemaphoreType.DMA,
            pltpu.SemaphoreType.DMA((2,)),
        ],
        compiler_params=pltpu.CompilerParams(
            collective_id=0, has_side_effects=True, vmem_limit_bytes=48 * 1024 * 1024),
        name="cluster_totals",
    )(embeddings, labels.reshape(8, 128))
    return jnp.log1p(totals.reshape(DOCS_DEV))


def solution(mesh):
    return jax.shard_map(
        local,
        mesh=mesh,
        in_specs=(P("shard", None), P("shard")),
        out_specs=P("shard"),
        check_vma=False,
    )
```

time: 252 us -> 89.6 us (0.36)
  waiting for transfers between devices: 106 us -> 0 us
  Pallas kernels: 0 us -> 86.6 us
  local copies, waits for them, and re-layouts: 86.3 us -> 2.88 us
  starting transfers between devices: 36.3 us -> 0 us
  other arithmetic: 14.5 us -> 0 us
  blocking collectives: 5.53 us -> 0 us
    all_to_all x3 -> x0, waiting for transfers between devices: 106 us -> none  [the longest x1 95.6 us: local(): lax.all_to_all(outgoing, 'shard', split_axis=1, concat_axis=1, tiled=True)]
    pallas_call x0 -> x1, Pallas kernels: none -> 86.6 us  [local(): pl.pallas_call(kernel, out_shape=jax.ShapeDtypeStruct((8, 128), jnp.float...]
    gather x13 -> x0, local copies, waits for them, and re-layouts: 62.3 us -> none  [the longest x11 49.8 us: slot_ranks(): first_seen = jnp.searchsorted(sorted_labels, sorted_labels, side='left')]
    all_to_all x3 -> x0, starting transfers between devices: 36.3 us -> none  [the longest x1 16.5 us: local(): lax.all_to_all(presence, 'shard', split_axis=1, concat_axis=1, tiled=True)]
    scatter x2 -> x0, local copies, waits for them, and re-layouts: 10.7 us -> none  [the longest x1 6.43 us: local(): outgoing = jnp.zeros((CL_DEV, shard_count * slot_count, width), jnp.bfloa...]
    unnamed x6 -> x0, other arithmetic: 8.51 us -> none
    all_gather x1 -> x0, blocking collectives: 5.53 us -> none  [local(): densities = lax.all_gather(partial_sums, 'rep', axis=0, tiled=True)]
    unnamed x11 -> x4, local copies, waits for them, and re-layouts: 7.69 us -> 2.28 us
  transfers between devices with their start and end apart: 3 -> 0, of which waited for: 2 -> 0; matrix products, arithmetic and copies ran while one was open for 6% -> 0% of each run, Pallas kernels for 0% -> 0%
where the time goes in v1:
time: 89.6 us; the launch traced here: 89.5 us
  Pallas kernels  86.6 us (97%)
  local copies, waits for them, and re-layouts  2.88 us (3%)
    pallas_call x1, Pallas kernels, local(): pl.pallas_call(kernel, out_shape=jax.ShapeDtypeStruct((8, 128), jnp.float...  86.6 us
    unnamed x4, local copies, waits for them, and re-layouts  2.28 us

profile of v1, /device:TPU:1, one launch (start us, length us, event | category | flops | bytes accessed | tf_op | source)
XLA Modules:
  0.0 89.5 jit_solution(7338351283351027742)
XLA Ops:
  0.0 0.0 copy-start
  0.0 1.6 %copy-done = bf16[1024,1024]{1,0:T(8,128)(2,1)S(1)} copy-done((bf16[1024,1024]{1,0:T(8,128)(2,1)S(1)}, bf16[1024,1024]{1,0:T(8,128)(2,1)}, u32[]{:S(2)}) %copy-start) | copy-done | bytes 2097176
  1.6 0.0 copy-start.1
  1.6 0.7 copy-done.1
  2.3 86.6 %cluster_totals.1 = f32[8,128]{1,0:T(8,128)S(1)} custom-call(bf16[1024,1024]{1,0:T(8,128)(2,1)S(1)} %copy-done, s32[8,128]{1,0:T(8,128)S(1)} %bitcast.3), custom_call_target="tpu_custom_call" | custom-call | tf_op jit(solution)/shard_map/cluster_totals/pallas_call | solution.py:165
  88.9 0.6 log-plus-one_bitcast_fusion
Async XLA Ops:
  0.0 1.6 %copy-start = (bf16[1024,1024]{1,0:T(8,128)(2,1)S(1)}, bf16[1024,1024]{1,0:T(8,128)(2,1)}, u32[]{:S(2)}) copy-start(bf16[1024,1024]{1,0:T(8,128)(2,1)} %e_hbm.1) | copy-start | bytes 6291460
  1.6 0.7 copy-start.1

commit v2 on v1

--- a/solution.py
+++ b/solution.py
@@ -161,8 +161,8 @@
     pltpu.make_async_copy(ret.at[everything], ret.at[everything], back_send).wait()
 
 
-def local(embeddings, labels):
-    totals = pl.pallas_call(
+def direct_totals(embeddings, labels):
+    return pl.pallas_call(
         kernel,
         out_shape=jax.ShapeDtypeStruct((8, 128), jnp.float32),
         in_specs=[pl.BlockSpec(memory_space=pl.ANY), pl.BlockSpec(memory_space=pltpu.VMEM)],
@@ -186,6 +186,265 @@
             collective_id=0, has_side_effects=True, vmem_limit_bytes=48 * 1024 * 1024),
         name="cluster_totals",
     )(embeddings, labels.reshape(8, 128))
+
+
+PLANE = 16
+DEPTH = 8
+SLOTS = PLANE * CL
+PACK = 96
+LAST = PACK - 1
+ORDER = (1, 7, 2, 6, 3, 5, 4)
+
+
+def prefix_rank(marks):
+    i = lax.broadcasted_iota(jnp.int32, (SLOTS, SLOTS), 0)
+    j = lax.broadcasted_iota(jnp.int32, (SLOTS, SLOTS), 1)
+    before = jnp.where(i < j, 1.0, 0.0).astype(jnp.bfloat16)
+    return jnp.dot(marks.astype(jnp.bfloat16), before, preferred_element_type=jnp.float32)
+
+
+def pack_matrix(mark, rank):
+    row = lax.broadcasted_iota(jnp.int32, (PACK, SLOTS), 0)
+    hit = (row == rank.astype(jnp.int32)) & (mark > 0.0) & (row < LAST)
+    return jnp.where(hit, 1.0, 0.0).astype(jnp.bfloat16)
+
+
+def mark_absent(rows, mark):
+    column = jnp.broadcast_to(mark, (SLOTS, SLOTS)).T
+    first = jnp.where(column > 0.0, rows[:, :SLOTS], jnp.nan)
+    return jnp.concatenate([first, rows[:, SLOTS:]], axis=1)
+
+
+def packed_kernel(e_hbm, labels_hbm, out_ref, e_ref, labels_ref, zs, zr, ps, pr, unit, tot, r1, s2, r2,
+                  load_sem, zss, zrs, pss, prs, r1s, r1r, r1c, r2s, r2r):
+    me = lax.axis_index("shard")
+    rep = lax.axis_index("rep")
+    y, x, z = me // 32, me // 8 % 4, me % 8
+    z_dev = [y * 32 + x * 8 + (z + d) % 8 for d in range(DEPTH)]
+    p_dev = [(y + p // 4) % 4 * 32 + (x + p % 4) % 4 * 8 + z for p in range(PLANE)]
+
+    load = pltpu.make_async_copy(e_hbm, e_ref, load_sem.at[0])
+    load.start()
+    load_labels = pltpu.make_async_copy(labels_hbm, labels_ref, load_sem.at[1])
+    load_labels.start()
+
+    barrier = pltpu.get_barrier_semaphore()
+    for d in range(1, DEPTH):
+        pl.semaphore_signal(barrier, inc=1, device_id={"shard": z_dev[d]})
+    for p in range(1, PLANE):
+        for r in range(2):
+            pl.semaphore_signal(barrier, inc=1, device_id={"shard": p_dev[p], "rep": r})
+    pl.semaphore_signal(barrier, inc=1, device_id={"rep": 1 - rep})
+    load_labels.wait()
+
+    labels = labels_ref[...]
+    owner = labels // 16
+    doc_p = (owner // 32 - y + 4) % 4 * 4 + (owner // 8 % 4 - x + 4) % 4
+    doc_z = (owner % 8 - z + 8) % 8
+    doc_rep = labels % 16 // 8
+    doc_slot = doc_p * CL + labels % 8
+    key = jnp.where(doc_rep == rep, doc_z * SLOTS + doc_slot, -1)
+
+    ids = lax.broadcasted_iota(jnp.int32, (SLOTS, 128), 0)
+
+    def place(d):
+        return jnp.concatenate(
+            [jnp.where(ids + d * SLOTS == key[j:j + 1, :], 1.0, 0.0).astype(jnp.bfloat16)
+             for j in range(8)], axis=1)
+
+    placed = [place(d) for d in range(DEPTH)]
+    ones = jnp.ones((16, DOCS_DEV), jnp.bfloat16)
+    marks = jnp.concatenate(
+        [lax.dot_general(ones, a, (((1,), (1,)), ((), ())),
+                         preferred_element_type=jnp.float32)[:1] for a in placed], axis=0)
+    ranks = prefix_rank(marks)
+    row_id = lax.broadcasted_iota(jnp.int32, (PACK, SLOTS), 0)
+
+    load.wait()
+    own = jnp.dot(placed[0], e_ref[...], preferred_element_type=jnp.float32)
+    own = mark_absent(own, marks[:1]).reshape(PLANE, CL, D).astype(jnp.bfloat16)
+    ps[0] = own
+    pr[0, 0] = own[0]
+    for group in ((1, 7), (2, 6), (3, 5), (4,)):
+        select = jnp.concatenate(
+            [jnp.dot(pack_matrix(marks[d:d + 1], ranks[d:d + 1]), placed[d],
+                     preferred_element_type=jnp.float32) for d in group], axis=0)
+        rows = jnp.dot(select.astype(jnp.bfloat16), e_ref[...], preferred_element_type=jnp.float32)
+        for i, d in enumerate(group):
+            part = rows[i * PACK:(i + 1) * PACK]
+            first = jnp.where(row_id == LAST, marks[d:d + 1], part[:, :SLOTS])
+            zs[d] = jnp.concatenate([first, part[:, SLOTS:]], axis=1).astype(jnp.bfloat16)
+
+    pl.semaphore_wait(barrier, DEPTH - 1 + 2 * PLANE - 1)
+
+    def z_copy(d):
+        return pltpu.make_async_remote_copy(
+            src_ref=zs.at[d], dst_ref=zr.at[d], send_sem=zss.at[d], recv_sem=zrs.at[d],
+            device_id={"shard": z_dev[d]})
+
+    def forward(d):
+        for p in range(1, PLANE):
+            pltpu.make_async_remote_copy(
+                src_ref=ps.at[d, p], dst_ref=pr.at[d, p], send_sem=pss.at[d], recv_sem=prs.at[d],
+                device_id={"shard": p_dev[p]}).start()
+
+    others = pl.ds(1, PLANE - 1)
+    for d in ORDER:
+        z_copy(d).start()
+    forward(0)
+
+    full = [jnp.zeros((1, SLOTS), jnp.float32)]
+
+    def expand(d):
+        pltpu.make_async_copy(zr.at[d], zr.at[d], zrs.at[d]).wait()
+        mark = zr[d, PACK - 16:PACK, :SLOTS].astype(jnp.float32)[15:16]
+        rank = prefix_rank(jnp.broadcast_to(mark, (16, SLOTS)))[:1]
+        full[0] = jnp.maximum(full[0], rank + mark)
+        rows = lax.dot_general(pack_matrix(mark, rank), zr[d], (((0,), (0,)), ((), ())),
+                               preferred_element_type=jnp.float32)
+        rows = mark_absent(rows, mark).reshape(PLANE, CL, D).astype(jnp.bfloat16)
+        ps[d] = rows
+        pr[d, 0] = rows[0]
+        forward(d)
+
+    i = lax.broadcasted_iota(jnp.int32, (SLOTS, SLOTS), 0)
+    j = lax.broadcasted_iota(jnp.int32, (SLOTS, SLOTS), 1)
+    same = i % CL == j % CL
+    same_off = same & (i != j)
+
+    def weights(a, b, mask):
+        gram = lax.dot_general(a, b, (((1,), (1,)), ((), ())),
+                               preferred_element_type=jnp.float32)
+        ok = mask & (gram == gram)
+        w = jnp.where(ok, jnp.exp(sharpness * (gram - 1.0)), 0.0)
+        return jnp.sum(w, axis=0, keepdims=True)
+
+    totals = {}
+    done = []
+
+    def process(d):
+        k = len(done)
+        pltpu.make_async_copy(pr.at[d, others], pr.at[d, others], prs.at[d]).wait()
+        values = pr[d].astype(jnp.float32).reshape(SLOTS, D)
+        scale = lax.rsqrt(jnp.sum(values * values, axis=1, keepdims=True) + epsilon)
+        mine = (values * scale).astype(jnp.bfloat16)
+        unit[k * SLOTS:(k + 1) * SLOTS] = mine
+        total = weights(mine, mine, same_off)
+        if k:
+            before = unit[:k * SLOTS]
+            total += weights(before, mine, jnp.concatenate([same] * k, axis=0))
+            rest = weights(mine, before, jnp.concatenate([same] * k, axis=1))
+            for n, e in enumerate(done):
+                totals[e] += rest[:, n * SLOTS:(n + 1) * SLOTS]
+        totals[d] = total
+        done.append(d)
+
+    expand(1)
+    expand(7)
+    process(0)
+    expand(2)
+    expand(6)
+    process(1)
+    process(7)
+    expand(3)
+    expand(5)
+    process(2)
+    process(6)
+    expand(4)
+    process(3)
+    process(5)
+    process(4)
+
+    table = jnp.concatenate([totals[d] for d in range(DEPTH)], axis=0)
+    table = jnp.where(jnp.max(full[0], axis=1, keepdims=True) > float(LAST), -1.0, table)
+    tot[...] = table
+
+    def back_one(p, r):
+        return pltpu.make_async_remote_copy(
+            src_ref=tot, dst_ref=r1.at[(4 - p // 4) % 4 * 4 + (4 - p % 4) % 4, rep], send_sem=r1s, recv_sem=r1r,
+            device_id={"shard": p_dev[p], "rep": r})
+
+    for p in range(1, PLANE):
+        for r in range(2):
+            back_one(p, r).start()
+    across = pltpu.make_async_remote_copy(
+        src_ref=tot, dst_ref=r1.at[0, rep], send_sem=r1c.at[0], recv_sem=r1c.at[1],
+        device_id={"rep": 1 - rep})
+    across.start()
+    r1[0, rep] = table
+    pltpu.make_async_copy(r1.at[others], r1.at[others], r1r).wait()
+    across.wait()
+
+    lane = lax.broadcasted_iota(jnp.int32, (DEPTH, SLOTS), 1)
+    sides = []
+    for r in range(2):
+        side = jnp.zeros((DEPTH, SLOTS), jnp.float32)
+        for p in range(PLANE):
+            side = jnp.where(lane // CL == p, r1[p, r], side)
+        sides.append(side)
+    for d in range(DEPTH):
+        line = jnp.concatenate([s[d:d + 1] for s in sides], axis=1)
+        s2[d] = line
+        if d == 0:
+            r2[0] = line
+        else:
+            pltpu.make_async_remote_copy(
+                src_ref=s2.at[d], dst_ref=r2.at[d], send_sem=r2s, recv_sem=r2r,
+                device_id={"shard": z_dev[(DEPTH - d) % DEPTH]}).start()
+    rest = pl.ds(1, DEPTH - 1)
+    pltpu.make_async_copy(r2.at[rest], r2.at[rest], r2r).wait()
+
+    value = jnp.zeros((8, 128), jnp.float32)
+    least = jnp.zeros((1, 2 * SLOTS), jnp.float32)
+    for d in range(DEPTH):
+        line = r2[d]
+        least = jnp.minimum(least, line)
+        for r in range(2):
+            wide = jnp.broadcast_to(line[:, r * SLOTS:(r + 1) * SLOTS], (8, 128))
+            found = jnp.take_along_axis(wide, doc_slot, axis=1)
+            value = jnp.where((doc_z == d) & (doc_rep == r), found, value)
+    out_ref[...] = jnp.where(jnp.min(least, axis=1, keepdims=True) < 0.0, -1.0, value)
+
+    for d in ORDER:
+        pltpu.make_async_copy(zs.at[d], zs.at[d], zss.at[d]).wait()
+    for d in range(DEPTH):
+        pltpu.make_async_copy(ps.at[d, others], ps.at[d, others], pss.at[d]).wait()
+    pltpu.make_async_copy(r1.at[others], r1.at[others], r1s).wait()
+    pltpu.make_async_copy(s2.at[rest], s2.at[rest], r2s).wait()
+
+
+def packed_totals(embeddings, labels):
+    dma = pltpu.SemaphoreType.DMA
+    return pl.pallas_call(
+        packed_kernel,
+        out_shape=jax.ShapeDtypeStruct((8, 128), jnp.float32),
+        in_specs=[pl.BlockSpec(memory_space=pl.ANY)] * 2,
+        out_specs=pl.BlockSpec(memory_space=pltpu.VMEM),
+        scratch_shapes=[
+            pltpu.VMEM((DOCS_DEV, D), jnp.bfloat16),
+            pltpu.VMEM((8, 128), jnp.int32),
+            pltpu.VMEM((DEPTH, PACK, D), jnp.bfloat16),
+            pltpu.VMEM((DEPTH, PACK, D), jnp.bfloat16),
+            pltpu.VMEM((DEPTH, PLANE, CL, D), jnp.bfloat16),
+            pltpu.VMEM((DEPTH, PLANE, CL, D), jnp.bfloat16),
+            pltpu.VMEM((DEPTH * SLOTS, D), jnp.bfloat16),
+            pltpu.VMEM((DEPTH, SLOTS), jnp.float32),
+            pltpu.VMEM((PLANE, 2, DEPTH, SLOTS), jnp.float32),
+            pltpu.VMEM((DEPTH, 1, 2 * SLOTS), jnp.float32),
+            pltpu.VMEM((DEPTH, 1, 2 * SLOTS), jnp.float32),
+            dma((2,)), dma((DEPTH,)), dma((DEPTH,)), dma((DEPTH,)), dma((DEPTH,)),
+            dma, dma, dma((2,)), dma, dma,
+        ],
+        compiler_params=pltpu.CompilerParams(
+            collective_id=1, has_side_effects=True, vmem_limit_bytes=60 * 1024 * 1024),
+        name="packed_totals",
+    )(embeddings, labels.reshape(8, 128))
+
+
+def local(embeddings, labels):
+    totals = packed_totals(embeddings, labels)
+    totals = lax.cond(
+        totals[0, 0] < 0.0, lambda: direct_totals(embeddings, labels), lambda: totals)
     return jnp.log1p(totals.reshape(DOCS_DEV))
 
 

time: 89.6 us -> 69.1 us (0.77)
  Pallas kernels: 86.6 us -> 66.9 us
  local copies, waits for them, and re-layouts: 2.88 us -> 1.12 us
    pallas_call x1, Pallas kernels: 86.6 us -> 66.9 us  [packed_totals(): pl.pallas_call(packed_kernel, out_shape=jax.ShapeDtypeStruct((8, 128), jn...]
    unnamed x4 -> x6, local copies, waits for them, and re-layouts: 2.28 us -> 0.59 us
where the time goes in v2:
time: 69.1 us; the launch traced here: 68.9 us
  Pallas kernels  66.9 us (97%)
  local copies, waits for them, and re-layouts  1.12 us (2%)
  between operations  0.7 us (1%)
    pallas_call x1, Pallas kernels, packed_totals(): pl.pallas_call(packed_kernel, out_shape=jax.ShapeDtypeStruct((8, 128), jn...  66.9 us

profile of v2, /device:TPU:1, one launch (start us, length us, event | category | flops | bytes accessed | tf_op | source)
XLA Modules:
  0.0 68.9 jit_solution(15224348300175691717)
XLA Ops:
  0.0 0.0 copy-start.1
  0.0 0.0 copy-start
  0.0 66.9 %packed_totals.1 = f32[8,128]{1,0:T(8,128)S(1)} custom-call(bf16[1024,1024]{1,0:T(8,128)(2,1)} %e_hbm.1, s32[8,128]{1,0:T(8,128)} %bitcast.7), custom_call_target="tpu_custom_call" | custom-call | tf_op jit(solution)/shard_map/packed_totals/pallas_call | solution.py:418
  66.9 0.5 slice.3
  68.1 0.0 copy-done.1
  68.1 0.0 copy-done
  68.1 0.2 conditional.1
  68.3 0.0 copy-start.2
  68.4 0.6 copy-done.2
  (1 shorter events, 0.0 us)
Async XLA Ops:
  0.0 68.1 %copy-start.1 = (s32[1024]{0:T(1024)S(1)}, s32[1024]{0:T(1024)}, u32[]{:S(2)}) copy-start(s32[1024]{0:T(1024)} %param.5) | copy-start | bytes 12292
  0.0 68.1 %copy-start = (bf16[1024,1024]{1,0:T(8,128)(2,1)S(1)}, bf16[1024,1024]{1,0:T(8,128)(2,1)}, u32[]{:S(2)}) copy-start(bf16[1024,1024]{1,0:T(8,128)(2,1)} %e_hbm.1) | copy-start | bytes 6291460
  68.3 0.6 copy-start.2

commit v3 on v2

--- a/solution.py
+++ b/solution.py
@@ -191,42 +191,40 @@
 PLANE = 16
 DEPTH = 8
 SLOTS = PLANE * CL
-PACK = 96
+CHIP_SLOTS = 2 * SLOTS
+PACK = 168
 LAST = PACK - 1
+HALF = D // 2
+PAIRS = ((1, 7), (2, 6), (3, 5), (4,))
 ORDER = (1, 7, 2, 6, 3, 5, 4)
 
 
 def prefix_rank(marks):
-    i = lax.broadcasted_iota(jnp.int32, (SLOTS, SLOTS), 0)
-    j = lax.broadcasted_iota(jnp.int32, (SLOTS, SLOTS), 1)
+    i = lax.broadcasted_iota(jnp.int32, (CHIP_SLOTS, CHIP_SLOTS), 0)
+    j = lax.broadcasted_iota(jnp.int32, (CHIP_SLOTS, CHIP_SLOTS), 1)
     before = jnp.where(i < j, 1.0, 0.0).astype(jnp.bfloat16)
     return jnp.dot(marks.astype(jnp.bfloat16), before, preferred_element_type=jnp.float32)
 
 
-def pack_matrix(mark, rank):
-    row = lax.broadcasted_iota(jnp.int32, (PACK, SLOTS), 0)
-    hit = (row == rank.astype(jnp.int32)) & (mark > 0.0) & (row < LAST)
-    return jnp.where(hit, 1.0, 0.0).astype(jnp.bfloat16)
-
-
 def mark_absent(rows, mark):
-    column = jnp.broadcast_to(mark, (SLOTS, SLOTS)).T
-    first = jnp.where(column > 0.0, rows[:, :SLOTS], jnp.nan)
-    return jnp.concatenate([first, rows[:, SLOTS:]], axis=1)
-
-
-def packed_kernel(e_hbm, labels_hbm, out_ref, e_ref, labels_ref, zs, zr, ps, pr, unit, tot, r1, s2, r2,
-                  load_sem, zss, zrs, pss, prs, r1s, r1r, r1c, r2s, r2r):
+    column = jnp.broadcast_to(mark, (128, CHIP_SLOTS)).T
+    first = jnp.where(column > 0.0, rows[:, :128], jnp.nan)
+    return jnp.concatenate([first, rows[:, 128:]], axis=1)
+
+
+def packed_kernel(e_hbm, labels_hbm, out_ref, flag_ref, e_ref, labels_ref, zs, zr, ps, pr, unit, tot,
+                  r1, s2, r2, load_sem, zss, zrs, pss, prs, psc, prc, r1s, r1r, r1c, r2s, r2r):
     me = lax.axis_index("shard")
     rep = lax.axis_index("rep")
     y, x, z = me // 32, me // 8 % 4, me % 8
     z_dev = [y * 32 + x * 8 + (z + d) % 8 for d in range(DEPTH)]
     p_dev = [(y + p // 4) % 4 * 32 + (x + p % 4) % 4 * 8 + z for p in range(PLANE)]
 
-    load = pltpu.make_async_copy(e_hbm, e_ref, load_sem.at[0])
-    load.start()
     load_labels = pltpu.make_async_copy(labels_hbm, labels_ref, load_sem.at[1])
     load_labels.start()
+    mine = pl.ds(pl.multiple_of(rep * HALF, HALF), HALF)
+    load = pltpu.make_async_copy(e_hbm.at[:, mine], e_ref, load_sem.at[0])
+    load.start()
 
     barrier = pltpu.get_barrier_semaphore()
     for d in range(1, DEPTH):
@@ -243,39 +241,28 @@
     doc_z = (owner % 8 - z + 8) % 8
     doc_rep = labels % 16 // 8
     doc_slot = doc_p * CL + labels % 8
-    key = jnp.where(doc_rep == rep, doc_z * SLOTS + doc_slot, -1)
-
-    ids = lax.broadcasted_iota(jnp.int32, (SLOTS, 128), 0)
-
-    def place(d):
+    doc_chip = doc_p * 16 + labels % 16
+    doc_hi = doc_chip // 128 * DEPTH + doc_z
+    doc_lo = doc_chip % 128
+
+    def onehot(count, index):
+        ids = lax.broadcasted_iota(jnp.int32, (count, 128), 0)
         return jnp.concatenate(
-            [jnp.where(ids + d * SLOTS == key[j:j + 1, :], 1.0, 0.0).astype(jnp.bfloat16)
+            [jnp.where(ids == index[j:j + 1, :], 1.0, 0.0).astype(jnp.bfloat16)
              for j in range(8)], axis=1)
 
-    placed = [place(d) for d in range(DEPTH)]
-    ones = jnp.ones((16, DOCS_DEV), jnp.bfloat16)
-    marks = jnp.concatenate(
-        [lax.dot_general(ones, a, (((1,), (1,)), ((), ())),
-                         preferred_element_type=jnp.float32)[:1] for a in placed], axis=0)
+    marks = lax.dot_general(onehot(2 * DEPTH, doc_hi), onehot(128, doc_lo),
+                            (((1,), (1,)), ((), ())), preferred_element_type=jnp.float32)
+    marks = jnp.concatenate([marks[:DEPTH], marks[DEPTH:]], axis=1)
     ranks = prefix_rank(marks)
-    row_id = lax.broadcasted_iota(jnp.int32, (PACK, SLOTS), 0)
-
-    load.wait()
-    own = jnp.dot(placed[0], e_ref[...], preferred_element_type=jnp.float32)
-    own = mark_absent(own, marks[:1]).reshape(PLANE, CL, D).astype(jnp.bfloat16)
-    ps[0] = own
-    pr[0, 0] = own[0]
-    for group in ((1, 7), (2, 6), (3, 5), (4,)):
-        select = jnp.concatenate(
-            [jnp.dot(pack_matrix(marks[d:d + 1], ranks[d:d + 1]), placed[d],
-                     preferred_element_type=jnp.float32) for d in group], axis=0)
-        rows = jnp.dot(select.astype(jnp.bfloat16), e_ref[...], preferred_element_type=jnp.float32)
-        for i, d in enumerate(group):
-            part = rows[i * PACK:(i + 1) * PACK]
-            first = jnp.where(row_id == LAST, marks[d:d + 1], part[:, :SLOTS])
-            zs[d] = jnp.concatenate([first, part[:, SLOTS:]], axis=1).astype(jnp.bfloat16)
-
-    pl.semaphore_wait(barrier, DEPTH - 1 + 2 * PLANE - 1)
+    doc_rank = jnp.zeros((8, 128), jnp.float32)
+    for h in range(2):
+        for d in range(DEPTH):
+            line = jnp.broadcast_to(ranks[d:d + 1, h * 128:(h + 1) * 128], (8, 128))
+            doc_rank = jnp.where(
+                doc_hi == h * DEPTH + d, jnp.take_along_axis(line, doc_lo, axis=1), doc_rank)
+    doc_rank = doc_rank.astype(jnp.int32)
+    row_id = lax.broadcasted_iota(jnp.int32, (PACK, CHIP_SLOTS), 0)
 
     def z_copy(d):
         return pltpu.make_async_remote_copy(
@@ -283,29 +270,54 @@
             device_id={"shard": z_dev[d]})
 
     def forward(d):
+        pltpu.make_async_remote_copy(
+            src_ref=ps.at[d, 0, 1 - rep], dst_ref=pr.at[d, 0, rep], send_sem=psc.at[d],
+            recv_sem=prc.at[d], device_id={"rep": 1 - rep}).start()
         for p in range(1, PLANE):
-            pltpu.make_async_remote_copy(
-                src_ref=ps.at[d, p], dst_ref=pr.at[d, p], send_sem=pss.at[d], recv_sem=prs.at[d],
-                device_id={"shard": p_dev[p]}).start()
+            for r in range(2):
+                pltpu.make_async_remote_copy(
+                    src_ref=ps.at[d, p, r], dst_ref=pr.at[d, p, rep], send_sem=pss.at[d],
+                    recv_sem=prs.at[d], device_id={"shard": p_dev[p], "rep": r}).start()
+
+    def spread(d, rows, mark):
+        rows = mark_absent(rows, mark).reshape(PLANE, 2, CL, HALF).astype(jnp.bfloat16)
+        ps[d] = rows
+        pr[d, 0, rep] = ps[d, 0, rep]
+        forward(d)
+
+    def pack(group):
+        select = jnp.concatenate(
+            [onehot(PACK, jnp.where(doc_z == d, doc_rank, -1)) for d in group], axis=0)
+        rows = jnp.dot(select, e_ref[...], preferred_element_type=jnp.float32)
+        for i, d in enumerate(group):
+            part = rows[i * PACK:(i + 1) * PACK]
+            first = jnp.where(row_id == LAST, marks[d:d + 1], part[:, :CHIP_SLOTS])
+            zs[d] = jnp.concatenate([first, part[:, CHIP_SLOTS:]], axis=1).astype(jnp.bfloat16)
+
+    load.wait()
+    pack(PAIRS[0])
+    pl.semaphore_wait(barrier, DEPTH - 1 + 2 * PLANE - 1)
+    for d in PAIRS[0]:
+        z_copy(d).start()
+    spread(0, jnp.dot(onehot(CHIP_SLOTS, jnp.where(doc_z == 0, doc_chip, -1)), e_ref[...],
+                      preferred_element_type=jnp.float32), marks[:1])
+    for group in PAIRS[1:]:
+        pack(group)
+        for d in group:
+            z_copy(d).start()
 
     others = pl.ds(1, PLANE - 1)
-    for d in ORDER:
-        z_copy(d).start()
-    forward(0)
-
-    full = [jnp.zeros((1, SLOTS), jnp.float32)]
+    full = [jnp.zeros((1, CHIP_SLOTS), jnp.float32)]
 
     def expand(d):
         pltpu.make_async_copy(zr.at[d], zr.at[d], zrs.at[d]).wait()
-        mark = zr[d, PACK - 16:PACK, :SLOTS].astype(jnp.float32)[15:16]
-        rank = prefix_rank(jnp.broadcast_to(mark, (16, SLOTS)))[:1]
+        mark = zr[d, PACK - 8:PACK, :CHIP_SLOTS].astype(jnp.float32)[7:8]
+        rank = prefix_rank(jnp.broadcast_to(mark, (16, CHIP_SLOTS)))[:1]
         full[0] = jnp.maximum(full[0], rank + mark)
-        rows = lax.dot_general(pack_matrix(mark, rank), zr[d], (((0,), (0,)), ((), ())),
-                               preferred_element_type=jnp.float32)
-        rows = mark_absent(rows, mark).reshape(PLANE, CL, D).astype(jnp.bfloat16)
-        ps[d] = rows
-        pr[d, 0] = rows[0]
-        forward(d)
+        hit = (row_id == rank.astype(jnp.int32)) & (mark > 0.0) & (row_id < LAST)
+        select = jnp.where(hit, 1.0, 0.0).astype(jnp.bfloat16)
+        spread(d, lax.dot_general(select, zr[d], (((0,), (0,)), ((), ())),
+                                  preferred_element_type=jnp.float32), mark)
 
     i = lax.broadcasted_iota(jnp.int32, (SLOTS, SLOTS), 0)
     j = lax.broadcasted_iota(jnp.int32, (SLOTS, SLOTS), 1)
@@ -325,15 +337,17 @@
     def process(d):
         k = len(done)
         pltpu.make_async_copy(pr.at[d, others], pr.at[d, others], prs.at[d]).wait()
-        values = pr[d].astype(jnp.float32).reshape(SLOTS, D)
-        scale = lax.rsqrt(jnp.sum(values * values, axis=1, keepdims=True) + epsilon)
-        mine = (values * scale).astype(jnp.bfloat16)
-        unit[k * SLOTS:(k + 1) * SLOTS] = mine
-        total = weights(mine, mine, same_off)
+        pltpu.make_async_copy(pr.at[d, 0, 1 - rep], pr.at[d, 0, 1 - rep], prc.at[d]).wait()
+        sides = [pr[d, :, f].astype(jnp.float32).reshape(SLOTS, HALF) for f in range(2)]
+        square = jnp.sum(sides[0] * sides[0] + sides[1] * sides[1], axis=1, keepdims=True)
+        scale = lax.rsqrt(square + epsilon)
+        new = jnp.concatenate([(v * scale).astype(jnp.bfloat16) for v in sides], axis=1)
+        unit[k * SLOTS:(k + 1) * SLOTS] = new
+        total = weights(new, new, same_off)
         if k:
             before = unit[:k * SLOTS]
-            total += weights(before, mine, jnp.concatenate([same] * k, axis=0))
-            rest = weights(mine, before, jnp.concatenate([same] * k, axis=1))
+            total += weights(before, new, jnp.concatenate([same] * k, axis=0))
+            rest = weights(new, before, jnp.concatenate([same] * k, axis=1))
             for n, e in enumerate(done):
                 totals[e] += rest[:, n * SLOTS:(n + 1) * SLOTS]
         totals[d] = total
@@ -359,14 +373,11 @@
     table = jnp.where(jnp.max(full[0], axis=1, keepdims=True) > float(LAST), -1.0, table)
     tot[...] = table
 
-    def back_one(p, r):
-        return pltpu.make_async_remote_copy(
-            src_ref=tot, dst_ref=r1.at[(4 - p // 4) % 4 * 4 + (4 - p % 4) % 4, rep], send_sem=r1s, recv_sem=r1r,
-            device_id={"shard": p_dev[p], "rep": r})
-
     for p in range(1, PLANE):
         for r in range(2):
-            back_one(p, r).start()
+            pltpu.make_async_remote_copy(
+                src_ref=tot, dst_ref=r1.at[(4 - p // 4) % 4 * 4 + (4 - p % 4) % 4, rep],
+                send_sem=r1s, recv_sem=r1r, device_id={"shard": p_dev[p], "rep": r}).start()
     across = pltpu.make_async_remote_copy(
         src_ref=tot, dst_ref=r1.at[0, rep], send_sem=r1c.at[0], recv_sem=r1c.at[1],
         device_id={"rep": 1 - rep})
@@ -403,12 +414,14 @@
             wide = jnp.broadcast_to(line[:, r * SLOTS:(r + 1) * SLOTS], (8, 128))
             found = jnp.take_along_axis(wide, doc_slot, axis=1)
             value = jnp.where((doc_z == d) & (doc_rep == r), found, value)
-    out_ref[...] = jnp.where(jnp.min(least, axis=1, keepdims=True) < 0.0, -1.0, value)
+    out_ref[...] = value
+    flag_ref[0] = jnp.where(jnp.min(least) < 0.0, 1, 0).astype(jnp.int32)
 
     for d in ORDER:
         pltpu.make_async_copy(zs.at[d], zs.at[d], zss.at[d]).wait()
     for d in range(DEPTH):
         pltpu.make_async_copy(ps.at[d, others], ps.at[d, others], pss.at[d]).wait()
+        pltpu.make_async_copy(ps.at[d, 0, 1 - rep], ps.at[d, 0, 1 - rep], psc.at[d]).wait()
     pltpu.make_async_copy(r1.at[others], r1.at[others], r1s).wait()
     pltpu.make_async_copy(s2.at[rest], s2.at[rest], r2s).wait()
 
@@ -417,23 +430,24 @@
     dma = pltpu.SemaphoreType.DMA
     return pl.pallas_call(
         packed_kernel,
-        out_shape=jax.ShapeDtypeStruct((8, 128), jnp.float32),
+        out_shape=(jax.ShapeDtypeStruct((8, 128), jnp.float32),
+                   jax.ShapeDtypeStruct((1,), jnp.int32)),
         in_specs=[pl.BlockSpec(memory_space=pl.ANY)] * 2,
-        out_specs=pl.BlockSpec(memory_space=pltpu.VMEM),
+        out_specs=(pl.BlockSpec(memory_space=pltpu.VMEM), pl.BlockSpec(memory_space=pltpu.SMEM)),
         scratch_shapes=[
-            pltpu.VMEM((DOCS_DEV, D), jnp.bfloat16),
+            pltpu.VMEM((DOCS_DEV, HALF), jnp.bfloat16),
             pltpu.VMEM((8, 128), jnp.int32),
-            pltpu.VMEM((DEPTH, PACK, D), jnp.bfloat16),
-            pltpu.VMEM((DEPTH, PACK, D), jnp.bfloat16),
-            pltpu.VMEM((DEPTH, PLANE, CL, D), jnp.bfloat16),
-            pltpu.VMEM((DEPTH, PLANE, CL, D), jnp.bfloat16),
+            pltpu.VMEM((DEPTH, PACK, HALF), jnp.bfloat16),
+            pltpu.VMEM((DEPTH, PACK, HALF), jnp.bfloat16),
+            pltpu.VMEM((DEPTH, PLANE, 2, CL, HALF), jnp.bfloat16),
+            pltpu.VMEM((DEPTH, PLANE, 2, CL, HALF), jnp.bfloat16),
             pltpu.VMEM((DEPTH * SLOTS, D), jnp.bfloat16),
             pltpu.VMEM((DEPTH, SLOTS), jnp.float32),
             pltpu.VMEM((PLANE, 2, DEPTH, SLOTS), jnp.float32),
             pltpu.VMEM((DEPTH, 1, 2 * SLOTS), jnp.float32),
             pltpu.VMEM((DEPTH, 1, 2 * SLOTS), jnp.float32),
             dma((2,)), dma((DEPTH,)), dma((DEPTH,)), dma((DEPTH,)), dma((DEPTH,)),
-            dma, dma, dma((2,)), dma, dma,
+            dma((DEPTH,)), dma((DEPTH,)), dma, dma, dma((2,)), dma, dma,
         ],
         compiler_params=pltpu.CompilerParams(
             collective_id=1, has_side_effects=True, vmem_limit_bytes=60 * 1024 * 1024),
@@ -442,9 +456,9 @@
 
 
 def local(embeddings, labels):
-    totals = packed_totals(embeddings, labels)
+    totals, overflow = packed_totals(embeddings, labels)
     totals = lax.cond(
-        totals[0, 0] < 0.0, lambda: direct_totals(embeddings, labels), lambda: totals)
+        overflow[0] > 0, lambda: direct_totals(embeddings, labels), lambda: totals)
     return jnp.log1p(totals.reshape(DOCS_DEV))
 
 

time: 69.1 us -> 63.8 us (0.923)
  Pallas kernels: 66.9 us -> 62.4 us
    pallas_call x1, Pallas kernels: 66.9 us -> 62.4 us  [packed_totals(): pl.pallas_call(packed_kernel, out_shape=(jax.ShapeDtypeStruct((8, 128), j...]
where the time goes in v3:
time: 63.8 us
  Pallas kernels  62.4 us (98%)
    pallas_call x1, Pallas kernels, packed_totals(): pl.pallas_call(packed_kernel, out_shape=(jax.ShapeDtypeStruct((8, 128), j...  62.4 us

profile of v3, /device:TPU:1, one launch (start us, length us, event | category | flops | bytes accessed | tf_op | source)
XLA Modules:
  0.0 63.8 jit_solution(13330159058350683583)
XLA Ops:
  0.0 0.0 copy-start.1
  0.0 0.0 copy-start
  0.0 62.4 %packed_totals.1 = (f32[8,128]{1,0:T(8,128)S(1)}, s32[1]{0:T(128)}) custom-call(bf16[1024,1024]{1,0:T(8,128)(2,1)} %e_hbm.1, s32[8,128]{1,0:T(8,128)} %bitcast.7), custom_call_target="tpu_custom_call" | custom-call | tf_op jit(solution)/shard_map/packed_totals/pallas_call | solution.py:431
  62.9 0.0 copy-done.1
  62.9 0.0 copy-done
  63.0 0.2 conditional.1
  63.2 0.0 copy-start.2
  63.2 0.6 copy-done.2
  (1 shorter events, 0.0 us)
Async XLA Ops:
  0.0 62.9 %copy-start.1 = (s32[1024]{0:T(1024)S(1)}, s32[1024]{0:T(1024)}, u32[]{:S(2)}) copy-start(s32[1024]{0:T(1024)} %param.5) | copy-start | bytes 12292
  0.0 62.9 %copy-start = (bf16[1024,1024]{1,0:T(8,128)(2,1)S(1)}, bf16[1024,1024]{1,0:T(8,128)(2,1)}, u32[]{:S(2)}) copy-start(bf16[1024,1024]{1,0:T(8,128)(2,1)} %e_hbm.1) | copy-start | bytes 6291460
  63.2 0.6 copy-start.2

commit v4 on v3

--- a/solution.py
+++ b/solution.py
@@ -192,11 +192,13 @@
 DEPTH = 8
 SLOTS = PLANE * CL
 CHIP_SLOTS = 2 * SLOTS
-PACK = 168
-LAST = PACK - 1
+PACK = 160
 HALF = D // 2
 PAIRS = ((1, 7), (2, 6), (3, 5), (4,))
 ORDER = (1, 7, 2, 6, 3, 5, 4)
+FAR_Z = (4, 3, 5, 2, 6, 1, 7)
+FAR_PARTS = ((10, 9, 11, 8), (6, 5, 7, 4), (14, 13, 15, 12), (2, 1, 3, 0))
+FAR_PLANE = (10, 9, 11, 6, 14, 8, 2, 5, 7, 13, 15, 4, 12, 1, 3)
 
 
 def prefix_rank(marks):
@@ -206,14 +208,17 @@
     return jnp.dot(marks.astype(jnp.bfloat16), before, preferred_element_type=jnp.float32)
 
 
-def mark_absent(rows, mark):
-    column = jnp.broadcast_to(mark, (128, CHIP_SLOTS)).T
+def mark_column(mark):
+    return jnp.broadcast_to(mark, (128, CHIP_SLOTS)).T
+
+
+def mark_absent(rows, column):
     first = jnp.where(column > 0.0, rows[:, :128], jnp.nan)
     return jnp.concatenate([first, rows[:, 128:]], axis=1)
 
 
-def packed_kernel(e_hbm, labels_hbm, out_ref, flag_ref, e_ref, labels_ref, zs, zr, ps, pr, unit, tot,
-                  r1, s2, r2, load_sem, zss, zrs, pss, prs, psc, prc, r1s, r1r, r1c, r2s, r2r):
+def packed_kernel(e_hbm, labels_hbm, out_ref, flag_ref, e_ref, labels_ref, zs, zr, ms, mr, ps, pr, unit, tot,
+                  r1, s2, r2, load_sem, mss, mrs, zss, zrs, pss, prs, psc, prc, r1s, r1r, r1c, r2s, r2r):
     me = lax.axis_index("shard")
     rep = lax.axis_index("rep")
     y, x, z = me // 32, me // 8 % 4, me % 8
@@ -227,11 +232,9 @@
     load.start()
 
     barrier = pltpu.get_barrier_semaphore()
-    for d in range(1, DEPTH):
-        pl.semaphore_signal(barrier, inc=1, device_id={"shard": z_dev[d]})
-    for p in range(1, PLANE):
+    for target in [z_dev[d] for d in FAR_Z] + [p_dev[p] for p in FAR_PLANE]:
         for r in range(2):
-            pl.semaphore_signal(barrier, inc=1, device_id={"shard": p_dev[p], "rep": r})
+            pl.semaphore_signal(barrier, inc=1, device_id={"shard": target, "rep": r})
     pl.semaphore_signal(barrier, inc=1, device_id={"rep": 1 - rep})
     load_labels.wait()
 
@@ -263,61 +266,76 @@
                 doc_hi == h * DEPTH + d, jnp.take_along_axis(line, doc_lo, axis=1), doc_rank)
     doc_rank = doc_rank.astype(jnp.int32)
     row_id = lax.broadcasted_iota(jnp.int32, (PACK, CHIP_SLOTS), 0)
+    for d in range(1, DEPTH):
+        ms[d] = marks[d:d + 1]
+
+    def mark_copy(d):
+        return pltpu.make_async_remote_copy(
+            src_ref=ms.at[d], dst_ref=mr.at[d], send_sem=mss, recv_sem=mrs,
+            device_id={"shard": z_dev[d]})
 
     def z_copy(d):
         return pltpu.make_async_remote_copy(
             src_ref=zs.at[d], dst_ref=zr.at[d], send_sem=zss.at[d], recv_sem=zrs.at[d],
             device_id={"shard": z_dev[d]})
 
-    def forward(d):
-        pltpu.make_async_remote_copy(
-            src_ref=ps.at[d, 0, 1 - rep], dst_ref=pr.at[d, 0, rep], send_sem=psc.at[d],
-            recv_sem=prc.at[d], device_id={"rep": 1 - rep}).start()
-        for p in range(1, PLANE):
+    def spread(d, part, rows, column):
+        low = part[-1] * 16
+        rows = mark_absent(rows, column[low:low + 64])
+        ps[d, part[-1]:part[-1] + 4] = rows.reshape(4, 2, CL, HALF).astype(jnp.bfloat16)
+        for p in part:
+            if p == 0:
+                pltpu.make_async_remote_copy(
+                    src_ref=ps.at[d, 0, 1 - rep], dst_ref=pr.at[d, 0, rep], send_sem=psc.at[d],
+                    recv_sem=prc.at[d], device_id={"rep": 1 - rep}).start()
+                pr[d, 0, rep] = ps[d, 0, rep]
+                continue
             for r in range(2):
                 pltpu.make_async_remote_copy(
                     src_ref=ps.at[d, p, r], dst_ref=pr.at[d, p, rep], send_sem=pss.at[d],
                     recv_sem=prs.at[d], device_id={"shard": p_dev[p], "rep": r}).start()
-
-    def spread(d, rows, mark):
-        rows = mark_absent(rows, mark).reshape(PLANE, 2, CL, HALF).astype(jnp.bfloat16)
-        ps[d] = rows
-        pr[d, 0, rep] = ps[d, 0, rep]
-        forward(d)
 
     def pack(group):
         select = jnp.concatenate(
             [onehot(PACK, jnp.where(doc_z == d, doc_rank, -1)) for d in group], axis=0)
         rows = jnp.dot(select, e_ref[...], preferred_element_type=jnp.float32)
         for i, d in enumerate(group):
-            part = rows[i * PACK:(i + 1) * PACK]
-            first = jnp.where(row_id == LAST, marks[d:d + 1], part[:, :CHIP_SLOTS])
-            zs[d] = jnp.concatenate([first, part[:, CHIP_SLOTS:]], axis=1).astype(jnp.bfloat16)
+            zs[d] = rows[i * PACK:(i + 1) * PACK].astype(jnp.bfloat16)
 
     load.wait()
     pack(PAIRS[0])
-    pl.semaphore_wait(barrier, DEPTH - 1 + 2 * PLANE - 1)
+    pl.semaphore_wait(barrier, 2 * (DEPTH - 1) + 2 * (PLANE - 1) + 1)
+    for d in FAR_Z:
+        mark_copy(d).start()
     for d in PAIRS[0]:
         z_copy(d).start()
-    spread(0, jnp.dot(onehot(CHIP_SLOTS, jnp.where(doc_z == 0, doc_chip, -1)), e_ref[...],
-                      preferred_element_type=jnp.float32), marks[:1])
+    rows = jnp.dot(onehot(CHIP_SLOTS, jnp.where(doc_z == 0, doc_chip, -1)), e_ref[...],
+                   preferred_element_type=jnp.float32)
+    column = mark_column(marks[:1])
+    for part in FAR_PARTS:
+        spread(0, part, rows[part[-1] * 16:part[-1] * 16 + 64], column)
     for group in PAIRS[1:]:
         pack(group)
         for d in group:
             z_copy(d).start()
 
     others = pl.ds(1, PLANE - 1)
-    full = [jnp.zeros((1, CHIP_SLOTS), jnp.float32)]
+    around = pl.ds(1, DEPTH - 1)
+    pltpu.make_async_copy(mr.at[around], mr.at[around], mrs).wait()
+    there = jnp.concatenate([jnp.zeros((1, CHIP_SLOTS), jnp.float32)]
+                            + [mr[d] for d in range(1, DEPTH)], axis=0)
+    ranks = prefix_rank(there)
+    full = jnp.max(ranks + there)
+    ranks = jnp.where(there > 0.0, ranks, -1.0).astype(jnp.int32)
 
     def expand(d):
+        select = jnp.where(row_id == ranks[d:d + 1], 1.0, 0.0).astype(jnp.bfloat16)
+        column = mark_column(there[d:d + 1])
         pltpu.make_async_copy(zr.at[d], zr.at[d], zrs.at[d]).wait()
-        mark = zr[d, PACK - 8:PACK, :CHIP_SLOTS].astype(jnp.float32)[7:8]
-        rank = prefix_rank(jnp.broadcast_to(mark, (16, CHIP_SLOTS)))[:1]
-        full[0] = jnp.maximum(full[0], rank + mark)
-        hit = (row_id == rank.astype(jnp.int32)) & (mark > 0.0) & (row_id < LAST)
-        select = jnp.where(hit, 1.0, 0.0).astype(jnp.bfloat16)
-        spread(d, lax.dot_general(select, zr[d], (((0,), (0,)), ((), ())),
-                                  preferred_element_type=jnp.float32), mark)
+        rows = lax.dot_general(select, zr[d], (((0,), (0,)), ((), ())),
+                               preferred_element_type=jnp.float32)
+        for part in FAR_PARTS:
+            spread(d, part, rows[part[-1] * 16:part[-1] * 16 + 64], column)
 
     i = lax.broadcasted_iota(jnp.int32, (SLOTS, SLOTS), 0)
     j = lax.broadcasted_iota(jnp.int32, (SLOTS, SLOTS), 1)
@@ -370,50 +388,48 @@
     process(4)
 
     table = jnp.concatenate([totals[d] for d in range(DEPTH)], axis=0)
-    table = jnp.where(jnp.max(full[0], axis=1, keepdims=True) > float(LAST), -1.0, table)
-    tot[...] = table
-
-    for p in range(1, PLANE):
+    table = jnp.where(full > float(PACK), -1.0, table)
+    for d in range(DEPTH):
+        tot[d] = table[d:d + 1]
+
+    for d in FAR_Z:
         for r in range(2):
             pltpu.make_async_remote_copy(
-                src_ref=tot, dst_ref=r1.at[(4 - p // 4) % 4 * 4 + (4 - p % 4) % 4, rep],
-                send_sem=r1s, recv_sem=r1r, device_id={"shard": p_dev[p], "rep": r}).start()
+                src_ref=tot.at[d], dst_ref=r1.at[d, rep], send_sem=r1s, recv_sem=r1r,
+                device_id={"shard": z_dev[(DEPTH - d) % DEPTH], "rep": r}).start()
     across = pltpu.make_async_remote_copy(
-        src_ref=tot, dst_ref=r1.at[0, rep], send_sem=r1c.at[0], recv_sem=r1c.at[1],
+        src_ref=tot.at[0], dst_ref=r1.at[0, rep], send_sem=r1c.at[0], recv_sem=r1c.at[1],
         device_id={"rep": 1 - rep})
     across.start()
-    r1[0, rep] = table
-    pltpu.make_async_copy(r1.at[others], r1.at[others], r1r).wait()
+    r1[0, rep] = table[:1]
+    pltpu.make_async_copy(r1.at[around], r1.at[around], r1r).wait()
     across.wait()
 
-    lane = lax.broadcasted_iota(jnp.int32, (DEPTH, SLOTS), 1)
-    sides = []
-    for r in range(2):
-        side = jnp.zeros((DEPTH, SLOTS), jnp.float32)
-        for p in range(PLANE):
-            side = jnp.where(lane // CL == p, r1[p, r], side)
-        sides.append(side)
-    for d in range(DEPTH):
-        line = jnp.concatenate([s[d:d + 1] for s in sides], axis=1)
-        s2[d] = line
-        if d == 0:
-            r2[0] = line
-        else:
-            pltpu.make_async_remote_copy(
-                src_ref=s2.at[d], dst_ref=r2.at[d], send_sem=r2s, recv_sem=r2r,
-                device_id={"shard": z_dev[(DEPTH - d) % DEPTH]}).start()
-    rest = pl.ds(1, DEPTH - 1)
-    pltpu.make_async_copy(r2.at[rest], r2.at[rest], r2r).wait()
+    lane = lax.broadcasted_iota(jnp.int32, (8, SLOTS), 1)
+    base = lax.broadcasted_iota(jnp.int32, (8, SLOTS), 0) * CL + lane % CL
+    blocks = [jnp.zeros((8, SLOTS), jnp.float32) for _ in range(2)]
+    for n in range(2 * DEPTH):
+        line = jnp.broadcast_to(r1[n // 2, n % 2], (8, SLOTS))
+        for h in range(2):
+            moved = jnp.take_along_axis(line, base + h * 64, axis=1)
+            blocks[h] = jnp.where(lane // CL == n, moved, blocks[h])
+    for p in (0,) + FAR_PLANE:
+        s2[p] = blocks[p // 8][p % 8:p % 8 + 1]
+    r2[0] = blocks[0][:1]
+    for p in FAR_PLANE:
+        pltpu.make_async_remote_copy(
+            src_ref=s2.at[p], dst_ref=r2.at[p], send_sem=r2s, recv_sem=r2r,
+            device_id={"shard": p_dev[(4 - p // 4) % 4 * 4 + (4 - p % 4) % 4]}).start()
+    pltpu.make_async_copy(r2.at[others], r2.at[others], r2r).wait()
 
     value = jnp.zeros((8, 128), jnp.float32)
-    least = jnp.zeros((1, 2 * SLOTS), jnp.float32)
-    for d in range(DEPTH):
-        line = r2[d]
+    least = jnp.zeros((1, SLOTS), jnp.float32)
+    doc_lane = doc_z * 16 + labels % 16
+    for p in range(PLANE):
+        line = r2[p]
         least = jnp.minimum(least, line)
-        for r in range(2):
-            wide = jnp.broadcast_to(line[:, r * SLOTS:(r + 1) * SLOTS], (8, 128))
-            found = jnp.take_along_axis(wide, doc_slot, axis=1)
-            value = jnp.where((doc_z == d) & (doc_rep == r), found, value)
+        found = jnp.take_along_axis(jnp.broadcast_to(line, (8, 128)), doc_lane, axis=1)
+        value = jnp.where(doc_p == p, found, value)
     out_ref[...] = value
     flag_ref[0] = jnp.where(jnp.min(least) < 0.0, 1, 0).astype(jnp.int32)
 
@@ -422,8 +438,9 @@
     for d in range(DEPTH):
         pltpu.make_async_copy(ps.at[d, others], ps.at[d, others], pss.at[d]).wait()
         pltpu.make_async_copy(ps.at[d, 0, 1 - rep], ps.at[d, 0, 1 - rep], psc.at[d]).wait()
-    pltpu.make_async_copy(r1.at[others], r1.at[others], r1s).wait()
-    pltpu.make_async_copy(s2.at[rest], s2.at[rest], r2s).wait()
+    pltpu.make_async_copy(ms.at[around], ms.at[around], mss).wait()
+    pltpu.make_async_copy(r1.at[around], r1.at[around], r1s).wait()
+    pltpu.make_async_copy(s2.at[others], s2.at[others], r2s).wait()
 
 
 def packed_totals(embeddings, labels):
@@ -439,14 +456,16 @@
             pltpu.VMEM((8, 128), jnp.int32),
             pltpu.VMEM((DEPTH, PACK, HALF), jnp.bfloat16),
             pltpu.VMEM((DEPTH, PACK, HALF), jnp.bfloat16),
+            pltpu.VMEM((DEPTH, 1, CHIP_SLOTS), jnp.float32),
+            pltpu.VMEM((DEPTH, 1, CHIP_SLOTS), jnp.float32),
             pltpu.VMEM((DEPTH, PLANE, 2, CL, HALF), jnp.bfloat16),
             pltpu.VMEM((DEPTH, PLANE, 2, CL, HALF), jnp.bfloat16),
             pltpu.VMEM((DEPTH * SLOTS, D), jnp.bfloat16),
-            pltpu.VMEM((DEPTH, SLOTS), jnp.float32),
-            pltpu.VMEM((PLANE, 2, DEPTH, SLOTS), jnp.float32),
-            pltpu.VMEM((DEPTH, 1, 2 * SLOTS), jnp.float32),
-            pltpu.VMEM((DEPTH, 1, 2 * SLOTS), jnp.float32),
-            dma((2,)), dma((DEPTH,)), dma((DEPTH,)), dma((DEPTH,)), dma((DEPTH,)),
+            pltpu.VMEM((DEPTH, 1, SLOTS), jnp.float32),
+            pltpu.VMEM((DEPTH, 2, 1, SLOTS), jnp.float32),
+            pltpu.VMEM((PLANE, 1, SLOTS), jnp.float32),
+            pltpu.VMEM((PLANE, 1, SLOTS), jnp.float32),
+            dma((2,)), dma, dma, dma((DEPTH,)), dma((DEPTH,)), dma((DEPTH,)), dma((DEPTH,)),
             dma((DEPTH,)), dma((DEPTH,)), dma, dma, dma((2,)), dma, dma,
         ],
         compiler_params=pltpu.CompilerParams(

time: 63.8 us -> 60.7 us (0.951)
  Pallas kernels: 62.4 us -> 59.2 us
    pallas_call x1, Pallas kernels: 62.4 us -> 59.2 us  [packed_totals(): pl.pallas_call(packed_kernel, out_shape=(jax.ShapeDtypeStruct((8, 128), j...]
where the time goes in v4:
time: 60.7 us; the launch traced here: 60.6 us
  Pallas kernels  59.2 us (98%)
    pallas_call x1, Pallas kernels, packed_totals(): pl.pallas_call(packed_kernel, out_shape=(jax.ShapeDtypeStruct((8, 128), j...  59.2 us

profile of v4, /device:TPU:1, one launch (start us, length us, event | category | flops | bytes accessed | tf_op | source)
XLA Modules:
  0.0 60.6 jit_solution(10504516372266395985)
XLA Ops:
  0.0 0.0 copy-start.1
  0.0 0.0 copy-start
  0.0 59.2 %packed_totals.1 = (f32[8,128]{1,0:T(8,128)S(1)}, s32[1]{0:T(128)}) custom-call(bf16[1024,1024]{1,0:T(8,128)(2,1)} %e_hbm.1, s32[8,128]{1,0:T(8,128)} %bitcast.7), custom_call_target="tpu_custom_call" | custom-call | tf_op jit(solution)/shard_map/packed_totals/pallas_call | solution.py:448
  59.8 0.0 copy-done.1
  59.8 0.0 copy-done
  59.8 0.2 conditional.1
  60.0 0.0 copy-start.2
  60.1 0.6 copy-done.2
  (1 shorter events, 0.0 us)
Async XLA Ops:
  0.0 59.8 %copy-start.1 = (s32[1024]{0:T(1024)S(1)}, s32[1024]{0:T(1024)}, u32[]{:S(2)}) copy-start(s32[1024]{0:T(1024)} %param.5) | copy-start | bytes 12292
  0.0 59.8 %copy-start = (bf16[1024,1024]{1,0:T(8,128)(2,1)S(1)}, bf16[1024,1024]{1,0:T(8,128)(2,1)}, u32[]{:S(2)}) copy-start(bf16[1024,1024]{1,0:T(8,128)(2,1)} %e_hbm.1) | copy-start | bytes 6291460
  60.0 0.6 copy-start.2

commit v5 on v4

--- a/solution.py
+++ b/solution.py
@@ -213,7 +213,7 @@
 
 
 def mark_absent(rows, column):
-    first = jnp.where(column > 0.0, rows[:, :128], jnp.nan)
+    first = jnp.where(column >= 0, rows[:, :128], jnp.nan)
     return jnp.concatenate([first, rows[:, 128:]], axis=1)
 
 
@@ -303,21 +303,18 @@
             zs[d] = rows[i * PACK:(i + 1) * PACK].astype(jnp.bfloat16)
 
     load.wait()
-    pack(PAIRS[0])
+    for group in PAIRS:
+        pack(group)
     pl.semaphore_wait(barrier, 2 * (DEPTH - 1) + 2 * (PLANE - 1) + 1)
     for d in FAR_Z:
         mark_copy(d).start()
-    for d in PAIRS[0]:
+    for d in ORDER:
         z_copy(d).start()
     rows = jnp.dot(onehot(CHIP_SLOTS, jnp.where(doc_z == 0, doc_chip, -1)), e_ref[...],
                    preferred_element_type=jnp.float32)
-    column = mark_column(marks[:1])
+    column = mark_column(jnp.where(marks[:1] > 0.0, 0, -1))
     for part in FAR_PARTS:
         spread(0, part, rows[part[-1] * 16:part[-1] * 16 + 64], column)
-    for group in PAIRS[1:]:
-        pack(group)
-        for d in group:
-            z_copy(d).start()
 
     others = pl.ds(1, PLANE - 1)
     around = pl.ds(1, DEPTH - 1)
@@ -328,12 +325,14 @@
     full = jnp.max(ranks + there)
     ranks = jnp.where(there > 0.0, ranks, -1.0).astype(jnp.int32)
 
+    place = lax.broadcasted_iota(jnp.int32, (CHIP_SLOTS, PACK), 1)
+
     def expand(d):
-        select = jnp.where(row_id == ranks[d:d + 1], 1.0, 0.0).astype(jnp.bfloat16)
-        column = mark_column(there[d:d + 1])
+        column = mark_column(ranks[d:d + 1])
+        wide = jnp.concatenate([column, column[:, :PACK - 128]], axis=1)
+        select = jnp.where(place == wide, 1.0, 0.0).astype(jnp.bfloat16)
         pltpu.make_async_copy(zr.at[d], zr.at[d], zrs.at[d]).wait()
-        rows = lax.dot_general(select, zr[d], (((0,), (0,)), ((), ())),
-                               preferred_element_type=jnp.float32)
+        rows = jnp.dot(select, zr[d], preferred_element_type=jnp.float32)
         for part in FAR_PARTS:
             spread(d, part, rows[part[-1] * 16:part[-1] * 16 + 64], column)
 
@@ -342,12 +341,11 @@
     same = i % CL == j % CL
     same_off = same & (i != j)
 
-    def weights(a, b, mask):
+    def masked(a, b, mask):
         gram = lax.dot_general(a, b, (((1,), (1,)), ((), ())),
                                preferred_element_type=jnp.float32)
         ok = mask & (gram == gram)
-        w = jnp.where(ok, jnp.exp(sharpness * (gram - 1.0)), 0.0)
-        return jnp.sum(w, axis=0, keepdims=True)
+        return jnp.where(ok, jnp.exp(sharpness * (gram - 1.0)), 0.0)
 
     totals = {}
     done = []
@@ -361,14 +359,12 @@
         scale = lax.rsqrt(square + epsilon)
         new = jnp.concatenate([(v * scale).astype(jnp.bfloat16) for v in sides], axis=1)
         unit[k * SLOTS:(k + 1) * SLOTS] = new
-        total = weights(new, new, same_off)
-        if k:
-            before = unit[:k * SLOTS]
-            total += weights(before, new, jnp.concatenate([same] * k, axis=0))
-            rest = weights(new, before, jnp.concatenate([same] * k, axis=1))
-            for n, e in enumerate(done):
-                totals[e] += rest[:, n * SLOTS:(n + 1) * SLOTS]
-        totals[d] = total
+        both = jnp.concatenate([same] * k + [same_off], axis=0)
+        grid = masked(unit[:(k + 1) * SLOTS], new, both)
+        totals[d] = jnp.sum(grid, axis=0, keepdims=True)
+        for n, e in enumerate(done):
+            back = grid[n * SLOTS:(n + 1) * SLOTS].T
+            totals[e] += jnp.sum(back, axis=0, keepdims=True)
         done.append(d)
 
     expand(1)

time: 60.7 us -> 60.3 us (level)
  no operation moved by 1% of the time
where the time goes in v5:
time: 60.3 us
  Pallas kernels  58.9 us (98%)
    pallas_call x1, Pallas kernels, packed_totals(): pl.pallas_call(packed_kernel, out_shape=(jax.ShapeDtypeStruct((8, 128), j...  58.9 us

profile of v5, /device:TPU:1, one launch (start us, length us, event | category | flops | bytes accessed | tf_op | source)
XLA Modules:
  0.0 60.3 jit_solution(14835455623877963124)
XLA Ops:
  0.0 0.0 copy-start.1
  0.0 0.0 copy-start
  0.0 58.9 %packed_totals.1 = (f32[8,128]{1,0:T(8,128)S(1)}, s32[1]{0:T(128)}) custom-call(bf16[1024,1024]{1,0:T(8,128)(2,1)} %e_hbm.1, s32[8,128]{1,0:T(8,128)} %bitcast.7), custom_call_target="tpu_custom_call" | custom-call | tf_op jit(solution)/shard_map/packed_totals/pallas_call | solution.py:444
  59.4 0.0 copy-done.1
  59.4 0.0 copy-done
  59.4 0.2 conditional.1
  59.7 0.0 copy-start.2
  59.7 0.6 copy-done.2
  (1 shorter events, 0.0 us)
Async XLA Ops:
  0.0 59.4 %copy-start.1 = (s32[1024]{0:T(1024)S(1)}, s32[1024]{0:T(1024)}, u32[]{:S(2)}) copy-start(s32[1024]{0:T(1024)} %param.5) | copy-start | bytes 12292
  0.0 59.4 %copy-start = (bf16[1024,1024]{1,0:T(8,128)(2,1)S(1)}, bf16[1024,1024]{1,0:T(8,128)(2,1)}, u32[]{:S(2)}) copy-start(bf16[1024,1024]{1,0:T(8,128)(2,1)} %e_hbm.1) | copy-start | bytes 6291460
  59.7 0.6 copy-start.2

commit v6 on v5

--- a/solution.py
+++ b/solution.py
@@ -403,19 +403,28 @@
 
     lane = lax.broadcasted_iota(jnp.int32, (8, SLOTS), 1)
     base = lax.broadcasted_iota(jnp.int32, (8, SLOTS), 0) * CL + lane % CL
-    blocks = [jnp.zeros((8, SLOTS), jnp.float32) for _ in range(2)]
-    for n in range(2 * DEPTH):
-        line = jnp.broadcast_to(r1[n // 2, n % 2], (8, SLOTS))
-        for h in range(2):
+    for h, far in ((1, (10, 9, 11, 8, 14, 13, 15, 12)), (0, (6, 2, 5, 7, 4, 1, 3, 0))):
+        block = jnp.zeros((8, SLOTS), jnp.float32)
+        for n in range(2 * DEPTH):
+            line = jnp.broadcast_to(r1[n // 2, n % 2], (8, SLOTS))
             moved = jnp.take_along_axis(line, base + h * 64, axis=1)
-            blocks[h] = jnp.where(lane // CL == n, moved, blocks[h])
-    for p in (0,) + FAR_PLANE:
-        s2[p] = blocks[p // 8][p % 8:p % 8 + 1]
-    r2[0] = blocks[0][:1]
-    for p in FAR_PLANE:
-        pltpu.make_async_remote_copy(
-            src_ref=s2.at[p], dst_ref=r2.at[p], send_sem=r2s, recv_sem=r2r,
-            device_id={"shard": p_dev[(4 - p // 4) % 4 * 4 + (4 - p % 4) % 4]}).start()
+            block = jnp.where(lane // CL == n, moved, block)
+        for p in far:
+            s2[p] = block[p % 8:p % 8 + 1]
+        for p in far:
+            if p == 0:
+                r2[0] = block[:1]
+                continue
+            pltpu.make_async_remote_copy(
+                src_ref=s2.at[p], dst_ref=r2.at[p], send_sem=r2s, recv_sem=r2r,
+                device_id={"shard": p_dev[(4 - p // 4) % 4 * 4 + (4 - p % 4) % 4]}).start()
+    for d in ORDER:
+        pltpu.make_async_copy(zs.at[d], zs.at[d], zss.at[d]).wait()
+    for d in range(DEPTH):
+        pltpu.make_async_copy(ps.at[d, others], ps.at[d, others], pss.at[d]).wait()
+        pltpu.make_async_copy(ps.at[d, 0, 1 - rep], ps.at[d, 0, 1 - rep], psc.at[d]).wait()
+    pltpu.make_async_copy(ms.at[around], ms.at[around], mss).wait()
+    pltpu.make_async_copy(r1.at[around], r1.at[around], r1s).wait()
     pltpu.make_async_copy(r2.at[others], r2.at[others], r2r).wait()
 
     value = jnp.zeros((8, 128), jnp.float32)
@@ -429,13 +438,6 @@
     out_ref[...] = value
     flag_ref[0] = jnp.where(jnp.min(least) < 0.0, 1, 0).astype(jnp.int32)
 
-    for d in ORDER:
-        pltpu.make_async_copy(zs.at[d], zs.at[d], zss.at[d]).wait()
-    for d in range(DEPTH):
-        pltpu.make_async_copy(ps.at[d, others], ps.at[d, others], pss.at[d]).wait()
-        pltpu.make_async_copy(ps.at[d, 0, 1 - rep], ps.at[d, 0, 1 - rep], psc.at[d]).wait()
-    pltpu.make_async_copy(ms.at[around], ms.at[around], mss).wait()
-    pltpu.make_async_copy(r1.at[around], r1.at[around], r1s).wait()
     pltpu.make_async_copy(s2.at[others], s2.at[others], r2s).wait()
 
 

time: 60.3 us -> 60.3 us (level)
  no operation moved by 1% of the time
where the time goes in v6:
time: 60.3 us; the launch traced here: 60.2 us
  Pallas kernels  58.8 us (98%)
    pallas_call x1, Pallas kernels, packed_totals(): pl.pallas_call(packed_kernel, out_shape=(jax.ShapeDtypeStruct((8, 128), j...  58.8 us

profile of v6, /device:TPU:1, one launch (start us, length us, event | category | flops | bytes accessed | tf_op | source)
XLA Modules:
  0.0 60.2 jit_solution(17608081944833827280)
XLA Ops:
  0.0 0.0 copy-start.1
  0.0 0.0 copy-start
  0.0 58.8 %packed_totals.1 = (f32[8,128]{1,0:T(8,128)S(1)}, s32[1]{0:T(128)}) custom-call(bf16[1024,1024]{1,0:T(8,128)(2,1)} %e_hbm.1, s32[8,128]{1,0:T(8,128)} %bitcast.7), custom_call_target="tpu_custom_call" | custom-call | tf_op jit(solution)/shard_map/packed_totals/pallas_call | solution.py:446
  59.4 0.0 copy-done.1
  59.4 0.0 copy-done
  59.4 0.2 conditional.1
  59.6 0.0 copy-start.2
  59.6 0.6 copy-done.2
  (1 shorter events, 0.0 us)
Async XLA Ops:
  0.0 59.4 %copy-start.1 = (s32[1024]{0:T(1024)S(1)}, s32[1024]{0:T(1024)}, u32[]{:S(2)}) copy-start(s32[1024]{0:T(1024)} %param.5) | copy-start | bytes 12292
  0.0 59.4 %copy-start = (bf16[1024,1024]{1,0:T(8,128)(2,1)S(1)}, bf16[1024,1024]{1,0:T(8,128)(2,1)}, u32[]{:S(2)}) copy-start(bf16[1024,1024]{1,0:T(8,128)(2,1)} %e_hbm.1) | copy-start | bytes 6291460
  59.6 0.6 copy-start.2

commit v7 on v6

--- a/solution.py
+++ b/solution.py
@@ -225,17 +225,16 @@
     z_dev = [y * 32 + x * 8 + (z + d) % 8 for d in range(DEPTH)]
     p_dev = [(y + p // 4) % 4 * 32 + (x + p % 4) % 4 * 8 + z for p in range(PLANE)]
 
+    barrier = pltpu.get_barrier_semaphore()
+    for target in [z_dev[d] for d in FAR_Z] + [p_dev[p] for p in FAR_PLANE]:
+        for r in range(2):
+            pl.semaphore_signal(barrier, inc=1, device_id={"shard": target, "rep": r})
+    pl.semaphore_signal(barrier, inc=1, device_id={"rep": 1 - rep})
     load_labels = pltpu.make_async_copy(labels_hbm, labels_ref, load_sem.at[1])
     load_labels.start()
     mine = pl.ds(pl.multiple_of(rep * HALF, HALF), HALF)
     load = pltpu.make_async_copy(e_hbm.at[:, mine], e_ref, load_sem.at[0])
     load.start()
-
-    barrier = pltpu.get_barrier_semaphore()
-    for target in [z_dev[d] for d in FAR_Z] + [p_dev[p] for p in FAR_PLANE]:
-        for r in range(2):
-            pl.semaphore_signal(barrier, inc=1, device_id={"shard": target, "rep": r})
-    pl.semaphore_signal(barrier, inc=1, device_id={"rep": 1 - rep})
     load_labels.wait()
 
     labels = labels_ref[...]

time: 60.3 us -> 60.2 us (level)
  no operation moved by 1% of the time
where the time goes in v7:
time: 60.2 us; the launch traced here: 60.1 us
  Pallas kernels  58.7 us (98%)
    pallas_call x1, Pallas kernels, packed_totals(): pl.pallas_call(packed_kernel, out_shape=(jax.ShapeDtypeStruct((8, 128), j...  58.7 us

profile of v7, /device:TPU:1, one launch (start us, length us, event | category | flops | bytes accessed | tf_op | source)
XLA Modules:
  0.0 60.1 jit_solution(3514362652687928833)
XLA Ops:
  0.0 0.0 copy-start.1
  0.0 0.0 copy-start
  0.0 58.7 %packed_totals.1 = (f32[8,128]{1,0:T(8,128)S(1)}, s32[1]{0:T(128)}) custom-call(bf16[1024,1024]{1,0:T(8,128)(2,1)} %e_hbm.1, s32[8,128]{1,0:T(8,128)} %bitcast.7), custom_call_target="tpu_custom_call" | custom-call | tf_op jit(solution)/shard_map/packed_totals/pallas_call | solution.py:445
  59.3 0.0 copy-done.1
  59.3 0.0 copy-done
  59.3 0.2 conditional.1
  59.5 0.0 copy-start.2
  59.6 0.6 copy-done.2
  (1 shorter events, 0.0 us)
Async XLA Ops:
  0.0 59.3 %copy-start.1 = (s32[1024]{0:T(1024)S(1)}, s32[1024]{0:T(1024)}, u32[]{:S(2)}) copy-start(s32[1024]{0:T(1024)} %param.5) | copy-start | bytes 12292
  0.0 59.3 %copy-start = (bf16[1024,1024]{1,0:T(8,128)(2,1)S(1)}, bf16[1024,1024]{1,0:T(8,128)(2,1)}, u32[]{:S(2)}) copy-start(bf16[1024,1024]{1,0:T(8,128)(2,1)} %e_hbm.1) | copy-start | bytes 6291460
  59.5 0.6 copy-start.2
